TPU v7x, 512 devices: a whole 4x4x16 slice. The times are simulated.
512 devices in a mesh: pos: 128 (over z_lo, x, y, core), mode: 4 (over z_hi).
Axes of the slice: x: 4, y: 4, z: 16 (z_hi: 4, z_lo: 4; z = z_hi * 4 + z_lo), core: 2. Of those that a mesh axis runs over, the one named last changes fastest.
Arguments:
- object_field: float32 [2, 32768, 384], P(None, 'pos'), may hold values from -6 to 6
- probe: float32 [4, 2, 256, 256], P('mode'), may hold values from -3 to 3
- offsets: int32 [1024, 2], P('pos'), may hold values from 0 to 32767, as said below
- live: int32 [1024], P('pos'), may hold values from 0 to 1, as said below
- measured: float32 [1024, 256, 256], P('pos'), may hold values from 0.1 to 10
- gaps: int32 [256, 256], replicated, may hold values 0 or 1
Outputs:
- smoothed: float32 [2, 32768, 384], P(None, 'pos')
Inputs may be any that keep to these rules, and one draw needn't show every extreme that they name: `offsets`: position n's row offset lies in [(n // 8) * 256, (n // 8 + 1) * 256), its column offset in [0, 128]; on every index of pos both ends of both ranges are taken. Each index of pos holds a leading run of one to 8 live slots followed by dead ones; some index has all 8 live.
All inputs are finite; a program needn't handle non-finite values.
Results may differ from a plain program's by a relative error of at most 0.0001.
Values sent between devices are 32-bit elements; how exact they have to be, the bound alone decides.
A program may use at most 64 MiB of HBM per device.

v0:
```python
import math

import jax
import jax.numpy as jnp
from jax import lax
from jax.sharding import PartitionSpec as P

PATCH = 256


update_rate = 0.2
smooth_weight = 0.1
amplitude_floor = 0.25
gradient_soften = 0.25
highest = lax.Precision.HIGHEST


def from_behind(block, axis, distance):
    devices = range(lax.axis_size(axis))
    route = [(i - distance, i) for i in devices if i - distance in devices]
    return lax.ppermute(block, axis, route)


def with_halo(value, sides, width):
    for axis, dim in sides:
        size, length = (lax.axis_size(axis), value.shape[dim])
        up = [(i, (i + 1) % size) for i in range(size - 1)]
        down = [(j, i) for i, j in up]
        last = lax.slice_in_dim(value, length - width, length, axis=dim)
        initial = lax.slice_in_dim(value, 0, width, axis=dim)
        before = lax.ppermute(last, axis, up)
        after = lax.ppermute(initial, axis, down)
        value = jnp.concatenate([before, value, after], axis=dim)
    return value


def smooth(rimmed):
    grid = jnp.pad(rimmed, ((0, 0), (0, 0), (1, 1)))
    corner = grid[:, :-1, :-1]
    drow = grid[:, 1:, :-1] - corner
    dcol = grid[:, :-1, 1:] - corner
    mag = jnp.sqrt(jnp.sum(drow * drow + dcol * dcol, axis=0) + gradient_soften)
    vrow = drow / mag
    vcol = dcol / mag
    spread = vrow[:, 1:, 1:] - vrow[:, :-1, 1:] + vcol[:, 1:, 1:] - vcol[:, 1:, :-1]
    return rimmed[:, 1:-1, :] + smooth_weight * spread


def transform(real_part, imag_part, cosines, sines):
    left_real = jnp.einsum("jk,nkl->njl", cosines, real_part, precision=highest) + jnp.einsum(
        "jk,nkl->njl", sines, imag_part, precision=highest
    )
    left_imag = jnp.einsum("jk,nkl->njl", cosines, imag_part, precision=highest) - jnp.einsum(
        "jk,nkl->njl", sines, real_part, precision=highest
    )
    out_real = jnp.einsum("njk,kl->njl", left_real, cosines, precision=highest) + jnp.einsum(
        "njk,kl->njl", left_imag, sines, precision=highest
    )
    out_imag = jnp.einsum("njk,kl->njl", left_imag, cosines, precision=highest) - jnp.einsum(
        "njk,kl->njl", left_real, sines, precision=highest
    )
    return (out_real, out_imag)


def per_device(object_field, probe, offsets, live, measured, gaps):
    stripe = object_field.shape[1]
    width = object_field.shape[2]
    below = from_behind(object_field, "pos", -1)
    extended = jnp.concatenate([object_field, below], axis=1)
    all_rows = offsets[:, 0] - lax.axis_index("pos") * stripe
    all_cols = offsets[:, 1]

    def cut(row, col):
        return lax.dynamic_slice(extended, (jnp.int32(0), row, col), (2, PATCH, PATCH))

    index = jnp.arange(PATCH, dtype=jnp.int32)
    phase = (index[:, None] * index[None, :] % PATCH).astype(jnp.float32) * (2.0 * math.pi / PATCH)
    cosines = jnp.cos(phase) * PATCH ** (-0.5)
    sines = jnp.sin(phase) * PATCH ** (-0.5)
    mask = gaps.astype(jnp.float32)
    patches = jax.vmap(cut)(all_rows, all_cols)
    probe_real = probe[0, 0]
    probe_imag = probe[0, 1]
    patch_real = patches[:, 0]
    patch_imag = patches[:, 1]
    exit_real = probe_real * patch_real - probe_imag * patch_imag
    exit_imag = probe_real * patch_imag + probe_imag * patch_real
    spec_real, spec_imag = transform(exit_real, exit_imag, cosines, sines)
    local_power = spec_real * spec_real + spec_imag * spec_imag
    model = lax.psum(local_power, "mode")
    ratio = mask * jnp.sqrt(measured) / jnp.maximum(jnp.sqrt(model), amplitude_floor) + (1.0 - mask)
    back_real, back_imag = transform(ratio * spec_real, ratio * spec_imag, cosines, -sines)
    diff_real = back_real - exit_real
    diff_imag = back_imag - exit_imag
    alive = live.astype(jnp.float32)[:, None, None]
    grad_real = (probe_real * diff_real + probe_imag * diff_imag) * alive
    grad_imag = (probe_real * diff_imag - probe_imag * diff_real) * alive
    terms = jnp.stack([grad_real, grad_imag], axis=1)

    def place(slot, total):
        start = (jnp.int32(0), all_rows[slot], all_cols[slot])
        current = lax.dynamic_slice(total, start, (2, PATCH, PATCH))
        return lax.dynamic_update_slice(total, current + terms[slot], start)

    spread_grad = lax.fori_loop(
        0, terms.shape[0], place, jnp.zeros((2, 2 * stripe, width), jnp.float32)
    )
    summed = lax.psum(spread_grad, "mode")
    carried = from_behind(summed[:, stripe:], "pos", 1)
    owned = summed[:, :stripe] + carried
    updated = object_field + update_rate * owned
    rimmed = with_halo(updated, (("pos", 1),), 1)
    return smooth(rimmed)


def solution(mesh):
    return jax.shard_map(
        per_device,
        mesh=mesh,
        in_specs=(
            P(None, "pos", None),
            P("mode", None, None, None),
            P("pos", None),
            P("pos"),
            P("pos", None, None),
            P(),
        ),
        out_specs=P(None, "pos", None),
        check_vma=False,
    )
```

profile of v0, /device:TPU:63, one launch (start us, length us, event | category | flops | bytes accessed | tf_op | source)
XLA Modules:
  0.0 621.1 jit_solution(4179797094819084503)
XLA Ops:
  6.5 2.6 collective-permute-start
  9.1 0.8 compare_select_fusion.1
  9.9 1.1 slice_bitcast_fusion.1
  11.0 13.3 %collective-permute-done = f32[2,256,384]{2,1,0:T(8,128)S(1)} collective-permute-done((f32[2,256,384]{2,1,0:T(8,128)}, f32[2,256,384]{2,1,0:T(8,128)S(1)}, u32[]{:S(2)}, u32[]{:S(2)}) %collective-permute-start) | collective-permute-done | bytes 786464 | tf_op jit(solution)/shard_map/ppermute | solution.py:21
  24.3 1.2 pad_maximum_fusion.1
  25.5 24.4 %while.15 = (s32[]{:T(128)}, f32[2,512,384]{2,1,0:T(8,128)S(1)}, s32[8,3]{0,1:T(4,128)S(1)}, f32[8,2,256,256]{3,2,0,1:T(8,128)}, s32[]{:T(128)}) while((s32[]{:T(128)}, f32[2,512,384]{2,1,0:T(8,128)S(1)}, s32[8,3]{0,1:T(4,128)S(1)}, f32[8,2,256,256]{3,2,0,1:T(8,128)}, s32[]{:T(128)}) %tuple.52), condition=%wide.while_cond, body=%wide.while_body.sunk | while | flops 2 | bytes 1050217 | solution.py:74
  26.2 2.4 bitcast_dynamic-update-slice_fusion.2
  29.2 2.4 bitcast_dynamic-update-slice_fusion.2
  32.3 2.4 bitcast_dynamic-update-slice_fusion.2
  35.4 2.4 bitcast_dynamic-update-slice_fusion.2
  38.4 2.4 bitcast_dynamic-update-slice_fusion.2
  41.4 2.4 bitcast_dynamic-update-slice_fusion.2
  44.5 2.4 bitcast_dynamic-update-slice_fusion.2
  47.6 2.4 bitcast_dynamic-update-slice_fusion.2
  49.9 2.8 fusion.17
  52.7 4.4 fusion.58
  57.1 4.4 fusion.55
  61.4 4.9 convolution_subtract_fusion.1
  66.3 4.5 fusion.10
  70.8 4.5 fusion.8
  75.3 4.5 convolution_add_fusion.1
  79.8 4.5 fusion.18
  84.4 6.4 %multiply_add_fusion = (f32[8,256,256]{2,1,0:T(8,128)}, f32[8,256,256]{2,1,0:T(8,128)}) fusion(f32[8,256,256]{2,1,0:T(8,128)S(1)} %fusion.18, f32[8,256,256]{2,1,0:T(8,128)S(1)} %fusion.8, f32[8,256,256]{2,1,0:T(8,128)S(1)} %convolution_add_fusion.1), kind=kOutput, calls=%fused_computation.31 | convolution fusion | flops 1613692928 | bytes 10485760 | tf_op jit(solution)/shard_map/njk,kl->njl/dot_general | solution.py:59
  91.1 0.7 copy-done.8
  91.8 159.9 %all-reduce.4.cloned.1.call-done = f32[8,256,256]{2,1,0:T(8,128)} async-done(((f32[8,256,256]{2,1,0:T(8,128)}), f32[8,256,256]{2,1,0:T(8,128)}) %all-reduce.4.cloned.1.call-update) | async-done | bytes 2097168 | tf_op jit(solution)/shard_map/psum | solution.py:90
  251.7 3.7 divide_add_fusion
  255.4 4.5 fusion.33
  259.9 4.5 fusion.29
  264.5 4.9 convolution_subtract_fusion
  269.4 4.5 fusion
  273.9 4.5 fusion.2
  278.3 4.7 convolution_add_fusion
  283.1 4.5 subtract_subtract_fusion
  287.5 5.6 multiply_bitcast_fusion.1
  293.1 2.2 pad_maximum_fusion
  295.5 117.2 %while.14 = (s32[]{:T(128)}, f32[2,512,384]{2,1,0:T(8,128)S(1)}, s32[8]{0:T(128)S(1)}, s32[8]{0:T(128)S(1)}, f32[8,2,256,256]{3,2,0,1:T(8,128)}, /*index=5*/s32[]{:T(128)}, s32[]{:T(128)}, s32[]{:T(128)}, s32[]{:T(128)}) while((s32[]{:T(128)}, f32[2,512,384]{2,1,0:T(8,128)S(1)}, s32[8]{0:T(128)S(1)}, s32[8]{0:T(128)S(1)}, ...), condition=%wide.region_2.3_spmd, body=%wide.region_1.2_spmd.sunk | while | flops 131080 | bytes 2621641 | solution.py:105
  295.5 0.7 dynamic_slice.37
  298.2 0.7 dynamic_slice.36
  300.8 1.3 bitcast_add_fusion.2
  302.1 4.6 dynamic_update_slice.8
  306.7 0.7 dynamic_slice.37
  312.0 1.3 bitcast_add_fusion.2
  313.3 8.0 %dynamic_update_slice.8 = f32[2,512,384]{2,1,0:T(8,128)S(1)} dynamic-update-slice(f32[2,512,384]{2,1,0:T(8,128)S(1)} %get-tuple-element.234, f32[2,256,256]{2,1,0:T(8,128)S(1)} %bitcast_add_fusion.2, s32[]{:T(128)} %constant.65.clone.1..sunk, s32[]{:T(128)S(6)} %select_n.136, s32[]{:T(128)S(6)} %select_n.137) | dynamic-update-slice | bytes 1048580 | tf_op jit(solution)/shard_map/while/body/eval_jaxpr/dynamic_update_slice | solution.py:103
  326.7 1.3 bitcast_add_fusion.2
  328.0 9.3 %dynamic_update_slice.8 = f32[2,512,384]{2,1,0:T(8,128)S(1)} dynamic-update-slice(f32[2,512,384]{2,1,0:T(8,128)S(1)} %get-tuple-element.234, f32[2,256,256]{2,1,0:T(8,128)S(1)} %bitcast_add_fusion.2, s32[]{:T(128)} %constant.65.clone.1..sunk, s32[]{:T(128)S(6)} %select_n.136, s32[]{:T(128)S(6)} %select_n.137) | dynamic-update-slice | bytes 1048580 | tf_op jit(solution)/shard_map/while/body/eval_jaxpr/dynamic_update_slice | solution.py:103
  342.7 1.3 bitcast_add_fusion.2
  344.0 8.4 %dynamic_update_slice.8 = f32[2,512,384]{2,1,0:T(8,128)S(1)} dynamic-update-slice(f32[2,512,384]{2,1,0:T(8,128)S(1)} %get-tuple-element.234, f32[2,256,256]{2,1,0:T(8,128)S(1)} %bitcast_add_fusion.2, s32[]{:T(128)} %constant.65.clone.1..sunk, s32[]{:T(128)S(6)} %select_n.136, s32[]{:T(128)S(6)} %select_n.137) | dynamic-update-slice | bytes 1048580 | tf_op jit(solution)/shard_map/while/body/eval_jaxpr/dynamic_update_slice | solution.py:103
  357.7 1.3 bitcast_add_fusion.2
  359.0 8.5 %dynamic_update_slice.8 = f32[2,512,384]{2,1,0:T(8,128)S(1)} dynamic-update-slice(f32[2,512,384]{2,1,0:T(8,128)S(1)} %get-tuple-element.234, f32[2,256,256]{2,1,0:T(8,128)S(1)} %bitcast_add_fusion.2, s32[]{:T(128)} %constant.65.clone.1..sunk, s32[]{:T(128)S(6)} %select_n.136, s32[]{:T(128)S(6)} %select_n.137) | dynamic-update-slice | bytes 1048580 | tf_op jit(solution)/shard_map/while/body/eval_jaxpr/dynamic_update_slice | solution.py:103
  372.9 1.3 bitcast_add_fusion.2
  374.1 8.6 %dynamic_update_slice.8 = f32[2,512,384]{2,1,0:T(8,128)S(1)} dynamic-update-slice(f32[2,512,384]{2,1,0:T(8,128)S(1)} %get-tuple-element.234, f32[2,256,256]{2,1,0:T(8,128)S(1)} %bitcast_add_fusion.2, s32[]{:T(128)} %constant.65.clone.1..sunk, s32[]{:T(128)S(6)} %select_n.136, s32[]{:T(128)S(6)} %select_n.137) | dynamic-update-slice | bytes 1048580 | tf_op jit(solution)/shard_map/while/body/eval_jaxpr/dynamic_update_slice | solution.py:103
  388.1 1.3 bitcast_add_fusion.2
  389.4 8.7 %dynamic_update_slice.8 = f32[2,512,384]{2,1,0:T(8,128)S(1)} dynamic-update-slice(f32[2,512,384]{2,1,0:T(8,128)S(1)} %get-tuple-element.234, f32[2,256,256]{2,1,0:T(8,128)S(1)} %bitcast_add_fusion.2, s32[]{:T(128)} %constant.65.clone.1..sunk, s32[]{:T(128)S(6)} %select_n.136, s32[]{:T(128)S(6)} %select_n.137) | dynamic-update-slice | bytes 1048580 | tf_op jit(solution)/shard_map/while/body/eval_jaxpr/dynamic_update_slice | solution.py:103
  403.5 1.3 bitcast_add_fusion.2
  404.7 7.9 %dynamic_update_slice.8 = f32[2,512,384]{2,1,0:T(8,128)S(1)} dynamic-update-slice(f32[2,512,384]{2,1,0:T(8,128)S(1)} %get-tuple-element.234, f32[2,256,256]{2,1,0:T(8,128)S(1)} %bitcast_add_fusion.2, s32[]{:T(128)} %constant.65.clone.1..sunk, s32[]{:T(128)S(6)} %select_n.136, s32[]{:T(128)S(6)} %select_n.137) | dynamic-update-slice | bytes 1048580 | tf_op jit(solution)/shard_map/while/body/eval_jaxpr/dynamic_update_slice | solution.py:103
  412.7 1.1 copy-done.4
  413.8 151.4 %all-reduce.6.cloned.1.call-done = f32[2,512,384]{2,1,0:T(8,128)} async-done(((f32[2,512,384]{2,1,0:T(8,128)}), f32[2,512,384]{2,1,0:T(8,128)}) %all-reduce.6.cloned.1.call-update) | async-done | bytes 1572880 | tf_op jit(solution)/shard_map/psum | solution.py:108
  565.2 1.3 slice.84
  566.5 17.8 %collective-permute-start.1 = (f32[2,256,384]{2,1,0:T(8,128)S(1)}, f32[2,256,384]{2,1,0:T(8,128)S(1)}, u32[]{:S(2)}, u32[]{:S(2)}) collective-permute-start(f32[2,256,384]{2,1,0:T(8,128)S(1)} %slice.84), channel_id=1, source_target_pairs={{0,4},{4,8},{8,12},{12,16},{16,20},{20,24},{24,28},{28,32},{32,36}... | collective-permute-start | bytes 2359304 | tf_op jit(solution)/shard_map/ppermute | solution.py:21
  584.3 8.9 %collective-permute-done.1 = f32[2,256,384]{2,1,0:T(8,128)S(1)} collective-permute-done((f32[2,256,384]{2,1,0:T(8,128)S(1)}, f32[2,256,384]{2,1,0:T(8,128)S(1)}, u32[]{:S(2)}, u32[]{:S(2)}) %collective-permute-start.1) | collective-permute-done | bytes 786464 | tf_op jit(solution)/shard_map/ppermute | solution.py:21
  593.3 8.6 %collective-permute-start.2 = (f32[2,1,384]{2,1,0:T(1,128)S(1)}, f32[2,1,384]{2,1,0:T(1,128)S(1)}, u32[]{:S(2)}, u32[]{:S(2)}) collective-permute-start(f32[2,1,384]{2,1,0:T(1,128)S(1)} %get-tuple-element.139), channel_id=1, source_target_pairs={{0,4},{4,8},{8,12},{12,16},{16,20},{20,24},{24,28},{28,32},{32,36}... | collective-permute-start | bytes 9224 | tf_op jit(solution)/shard_map/ppermute | solution.py:31
  601.9 1.9 collective-permute-start.3
  603.9 7.2 %collective-permute-done.3 = f32[2,1,384]{2,1,0:T(1,128)S(1)} collective-permute-done((f32[2,1,384]{2,1,0:T(1,128)S(1)}, f32[2,1,384]{2,1,0:T(1,128)S(1)}, u32[]{:S(2)}, u32[]{:S(2)}) %collective-permute-start.3) | collective-permute-done | bytes 3104 | tf_op jit(solution)/shard_map/ppermute | solution.py:32
  612.5 1.6 fusion.36
  (65 shorter events, 15.9 us)
Async XLA Ops:
  6.5 245.2 %all-reduce.4.cloned.1.call-start = ((), (), s32[]{:S(2)}) async-start(), calls=%async_computation | async-start | bytes 4194304 | tf_op jit(solution)/shard_map/psum | solution.py:90
  6.5 17.7 %collective-permute-start = (f32[2,256,384]{2,1,0:T(8,128)}, f32[2,256,384]{2,1,0:T(8,128)S(1)}, u32[]{:S(2)}, u32[]{:S(2)}) collective-permute-start(f32[2,256,384]{2,1,0:T(8,128)} %param.8), channel_id=1, source_target_pairs={{4,0},{8,4},{12,8},{16,12},{20,16},{24,20},{28,24},{32,28},{36,32}... | collective-permute-start | bytes 2359304 | tf_op jit(solution)/shard_map/ppermute | solution.py:21
  52.7 22.6 %copy-start.2 = (f32[8,256,256]{2,1,0:T(8,128)}, f32[8,256,256]{2,1,0:T(8,128)S(1)}, u32[]{:S(2)}) copy-start(f32[8,256,256]{2,1,0:T(8,128)S(1)} %get-tuple-element.135) | copy-start | bytes 6291460
  84.4 6.5 %copy-start = (f32[8,256,256]{2,1,0:T(8,128)}, f32[8,256,256]{2,1,0:T(8,128)S(1)}, u32[]{:S(2)}) copy-start(f32[8,256,256]{2,1,0:T(8,128)S(1)} %fusion.18) | copy-start | bytes 6291460
  90.8 1.0 copy-start.8
  90.8 1.0 copy-start.9
  90.9 474.3 %all-reduce.6.cloned.1.call-start = ((), (), s32[]{:S(2)}) async-start(), calls=%async_computation.1 | async-start | bytes 3145728 | tf_op jit(solution)/shard_map/psum | solution.py:108
  251.7 3.7 copy-start.1
  255.4 4.5 copy-start.5
  278.3 4.7 copy-start.3
  412.7 1.1 copy-start.4
  412.7 180.5 %copy-start.6 = (f32[2,256,384]{2,1,0:T(8,128)S(1)}, f32[2,256,384]{2,1,0:T(8,128)}, u32[]{:S(2)}) copy-start(f32[2,256,384]{2,1,0:T(8,128)} %param.8) | copy-start | bytes 2359300
  565.2 28.0 %copy-start.7 = (f32[2,512,384]{2,1,0:T(8,128)S(1)}, f32[2,512,384]{2,1,0:T(8,128)}, u32[]{:S(2)}) copy-start(f32[2,512,384]{2,1,0:T(8,128)} %all-reduce.6.cloned.1.call-done) | copy-start | bytes 4718596
  566.5 26.7 %collective-permute-start.1 = (f32[2,256,384]{2,1,0:T(8,128)S(1)}, f32[2,256,384]{2,1,0:T(8,128)S(1)}, u32[]{:S(2)}, u32[]{:S(2)}) collective-permute-start(f32[2,256,384]{2,1,0:T(8,128)S(1)} %slice.84), channel_id=1, source_target_pairs={{0,4},{4,8},{8,12},{12,16},{16,20},{20,24},{24,28},{28,32},{32,36}... | collective-permute-start | bytes 2359304 | tf_op jit(solution)/shard_map/ppermute | solution.py:21
  593.3 10.5 %collective-permute-start.2 = (f32[2,1,384]{2,1,0:T(1,128)S(1)}, f32[2,1,384]{2,1,0:T(1,128)S(1)}, u32[]{:S(2)}, u32[]{:S(2)}) collective-permute-start(f32[2,1,384]{2,1,0:T(1,128)S(1)} %get-tuple-element.139), channel_id=1, source_target_pairs={{0,4},{4,8},{8,12},{12,16},{16,20},{20,24},{24,28},{28,32},{32,36}... | collective-permute-start | bytes 9224 | tf_op jit(solution)/shard_map/ppermute | solution.py:31
  601.9 9.1 %collective-permute-start.3 = (f32[2,1,384]{2,1,0:T(1,128)S(1)}, f32[2,1,384]{2,1,0:T(1,128)S(1)}, u32[]{:S(2)}, u32[]{:S(2)}) collective-permute-start(f32[2,1,384]{2,1,0:T(1,128)S(1)} %get-tuple-element.140), channel_id=1, source_target_pairs={{4,0},{8,4},{12,8},{16,12},{20,16},{24,20},{28,24},{32,28},{36,32}... | collective-permute-start | bytes 9224 | tf_op jit(solution)/shard_map/ppermute | solution.py:32
Sparse Core Ops, SparseCore 0:
  91.0 160.6 all-reduce.3
  413.9 151.1 all-reduce.5
where the time goes:
time: 631 us; the launch traced here: 621 us
  waiting for transfers between devices  341 us (54%)
  local copies, waits for them, and re-layouts  103 us (16%)
  matrix products  75.7 us (12%)
  loops' own time  32.7 us (5%)
  starting transfers between devices  31.1 us (5%)
  other arithmetic  23.9 us (4%)
  between operations  14 us (2%)
    psum x1, waiting for transfers between devices, per_device(): model = lax.psum(local_power, 'mode')  160 us
    psum x1, waiting for transfers between devices, per_device(): summed = lax.psum(spread_grad, 'mode')  151 us
    dynamic_update_slice x8, local copies, waits for them, and re-layouts, place(): return lax.dynamic_update_slice(total, current + terms[slot], start)  64 us
    another operation x1, loops' own time, per_device(): lax.fori_loop(0, terms.shape[0], place, jnp.zeros((2, 2 * stripe, width),...  32.6 us
    gather x24, local copies, waits for them, and re-layouts  24.4 us
    ppermute x2, waiting for transfers between devices, from_behind(): return lax.ppermute(block, axis, route)  22.2 us
    ppermute x2, starting transfers between devices, from_behind(): return lax.ppermute(block, axis, route)  20.3 us
  transfers between devices with their start and end apart: 6, of which 5 were waited for; matrix products, arithmetic and copies ran while one was open for 0% of the time, Pallas kernels for 0%

commit v1 on v0

v1 whole, which is shorter than its diff:
```python
import jax
import jax.numpy as jnp
import ml_dtypes
import numpy as np
from jax import lax
from jax.experimental import pallas as pl
from jax.experimental.pallas import tpu as pltpu
from jax.sharding import PartitionSpec as P

PATCH = 256
HALF = PATCH // 2
TALL = PATCH + 8
F32 = jnp.float32
BF16 = jnp.bfloat16
UPDATE_RATE = 0.2
SMOOTH_WEIGHT = 0.1
GRADIENT_SOFTEN = 0.25


def dft_tables():
    k = np.arange(HALF)
    rows = []
    for odd in (0, 1):
        angle = 2.0 * np.pi * ((k[:, None] * (2 * k[None, :] + odd)) % PATCH) / PATCH
        c, s = np.cos(angle) / 16.0, np.sin(angle) / 16.0
        w = np.block([[c, -s], [s, c]])
        for m in (w, w.T):
            hi = m.astype(ml_dtypes.bfloat16)
            lo = (m - hi.astype(np.float64)).astype(ml_dtypes.bfloat16)
            rows += [hi, lo]
    order = np.concatenate([np.arange(0, PATCH, 2), np.arange(1, PATCH, 2)])
    shuffle = np.zeros((PATCH, PATCH), ml_dtypes.bfloat16)
    shuffle[order, np.arange(PATCH)] = 1
    rows.append(shuffle)
    return np.stack(rows)


def halves(x):
    hi = x.astype(BF16)
    return hi, (x - hi.astype(F32)).astype(BF16)


def dot(a, b):
    return jnp.dot(a, b, preferred_element_type=F32)


def right(x, tab, at):
    hi, lo = halves(x)
    return dot(hi, tab[at]) + dot(hi, tab[at + 1]) + dot(lo, tab[at])


def left(tab, at, x):
    hi, lo = halves(x)
    return dot(tab[at], hi) + dot(tab[at + 1], hi) + dot(tab[at], lo)


WE, WET, WO, WOT, SHUF = 0, 2, 4, 6, 8


def forward(er, ei, tab):
    a, b = er[:, :HALF], er[:, HALF:]
    c, d = ei[:, :HALF], ei[:, HALF:]
    even = right(jnp.concatenate([a + b, c + d], 1), tab, WE)
    odd = right(jnp.concatenate([a - b, c - d], 1), tab, WO)
    yr = jnp.concatenate([even[:, :HALF], odd[:, :HALF]], 1)
    yi = jnp.concatenate([even[:, HALF:], odd[:, HALF:]], 1)
    s = jnp.concatenate([yr[:HALF] + yr[HALF:], yi[:HALF] + yi[HALF:]], 0)
    d = jnp.concatenate([yr[:HALF] - yr[HALF:], yi[:HALF] - yi[HALF:]], 0)
    return left(tab, WET, s), left(tab, WOT, d)


def inverse(te, to, tab):
    a = left(tab, WE, te)
    b = left(tab, WO, to)
    s, d = a + b, a - b
    zr = jnp.concatenate([s[:HALF], d[:HALF]], 0)
    zi = jnp.concatenate([s[HALF:], d[HALF:]], 0)
    a = right(jnp.concatenate([zr[:, :HALF], zi[:, :HALF]], 1), tab, WET)
    b = right(jnp.concatenate([zr[:, HALF:], zi[:, HALF:]], 1), tab, WOT)
    s, d = a + b, a - b
    outr = jnp.concatenate([s[:, :HALF], d[:, :HALF]], 1)
    outi = jnp.concatenate([s[:, HALF:], d[:, HALF:]], 1)
    return outr, outi


def unzip_rows(x, scr):
    scr[0] = x[:, :HALF]
    scr[1] = x[:, HALF:]
    pick = lambda at: jnp.concatenate([scr[0, pl.ds(at, HALF, 2), :], scr[1, pl.ds(at, HALF, 2), :]], 1)
    return pick(0), pick(1)


def grad_kernel(rows, cols, live, obj, halo, probe, meas, gaps, tab, acc, ext, spec, mask, scr):
    n = pl.program_id(0)
    modes = probe.shape[0]
    width = obj.shape[2]

    @pl.when(n == 0)
    def _():
        acc[...] = jnp.zeros_like(acc)
        ext[:, :PATCH] = obj[...]
        ext[:, PATCH:] = halo[...]
        even, odd = unzip_rows(dot(gaps[...].astype(F32).astype(BF16), tab[SHUF]), scr)
        mask[:HALF] = even
        mask[HALF:] = odd

    @pl.when(live[n] > 0)
    def _():
        col = cols[n]
        base = pl.multiple_of(rows[n] // 8 * 8, 8)
        down = rows[n] - base
        back = lax.rem(width - col, width)
        up = lax.rem(TALL - down, TALL)

        def cut(part):
            window = pltpu.roll(ext[part, pl.ds(base, TALL), :], back, 1)[:, :PATCH]
            return pltpu.roll(window, up, 0)[:PATCH]

        def put(part, value):
            value = jnp.concatenate([value, jnp.zeros((TALL - PATCH, PATCH), F32)], 0)
            value = pltpu.roll(value, down, 0)
            value = jnp.concatenate([value, jnp.zeros((TALL, width - PATCH), F32)], 1)
            acc[part, pl.ds(base, TALL), :] += pltpu.roll(value, col, 1)

        pr = cut(0)
        pi = cut(1)
        me = md = 0.0
        for m in range(modes):
            br, bi = probe[m, 0], probe[m, 1]
            e, o = forward(br * pr - bi * pi, br * pi + bi * pr, tab)
            spec[m, 0] = e
            spec[m, 1] = o
            me = me + (e[:HALF] * e[:HALF] + e[HALF:] * e[HALF:])
            md = md + (o[:HALF] * o[:HALF] + o[HALF:] * o[HALF:])
        root = jnp.sqrt(meas[0])
        hi, lo = halves(root)
        even, odd = unzip_rows(dot(hi, tab[SHUF]) + dot(lo, tab[SHUF]), scr)
        re = mask[:HALF] * (even * lax.rsqrt(jnp.maximum(me, 0.0625)) - 1.0)
        ro = mask[HALF:] * (odd * lax.rsqrt(jnp.maximum(md, 0.0625)) - 1.0)
        re = jnp.concatenate([re, re], 0)
        ro = jnp.concatenate([ro, ro], 0)
        gr = gi = 0.0
        for m in range(modes):
            zr, zi = inverse(spec[m, 0] * re, spec[m, 1] * ro, tab)
            br, bi = probe[m, 0], probe[m, 1]
            gr = gr + (br * zr + bi * zi)
            gi = gi + (br * zi - bi * zr)
        put(0, gr)
        put(1, gi)


def gradient(obj, halo, probe, rows, cols, live, meas, gaps):
    slots = meas.shape[0]
    stripe, width = obj.shape[1], obj.shape[2]
    tab = jnp.asarray(dft_tables())
    whole = lambda a: pl.BlockSpec(a.shape, lambda n, *_: (0,) * a.ndim)
    return pl.pallas_call(
        grad_kernel,
        out_shape=jax.ShapeDtypeStruct((2, 2 * stripe, width), F32),
        grid_spec=pltpu.PrefetchScalarGridSpec(
            num_scalar_prefetch=3,
            grid=(slots,),
            in_specs=[
                whole(obj),
                whole(halo),
                whole(probe),
                pl.BlockSpec((1, PATCH, PATCH), lambda n, *_: (n, 0, 0)),
                whole(gaps),
                whole(tab),
            ],
            out_specs=pl.BlockSpec((2, 2 * stripe, width), lambda n, *_: (0, 0, 0)),
            scratch_shapes=[
                pltpu.VMEM((2, 2 * stripe, width), F32),
                pltpu.VMEM((probe.shape[0], 2, PATCH, PATCH), F32),
                pltpu.VMEM((PATCH, PATCH), F32),
                pltpu.VMEM((2, PATCH, HALF), F32),
            ],
        ),
        compiler_params=pltpu.CompilerParams(vmem_limit_bytes=56 * 2**20),
    )(rows, cols, live, obj, halo, probe, meas, gaps, tab)


def smooth_kernel(obj, own, carried, above, below, out, grid):
    width = out.shape[2]
    rows = out.shape[1]
    grid[...] = jnp.zeros_like(grid)
    grid[:, 0:8, :width] = above[...]
    grid[:, 8 : rows + 8, :width] = obj[...] + UPDATE_RATE * (own[...] + carried[...])
    grid[:, rows + 8 : rows + 16, :width] = below[...]
    total = GRADIENT_SOFTEN
    pairs = []
    for part in (0, 1):
        u = grid[part]
        drow = pltpu.roll(u, u.shape[0] - 1, 0) - u
        dcol = pltpu.roll(u, u.shape[1] - 1, 1) - u
        total = total + drow * drow + dcol * dcol
        pairs.append((u, drow, dcol))
    inv = lax.rsqrt(total)
    for part, (u, drow, dcol) in enumerate(pairs):
        vrow, vcol = drow * inv, dcol * inv
        spread = vrow - pltpu.roll(vrow, 1, 0) + vcol - pltpu.roll(vcol, 1, 1)
        out[part] = (u + SMOOTH_WEIGHT * spread)[8 : rows + 8, :width]


def smoothed(obj, own, carried, above, below):
    rows, width = obj.shape[1:]
    return pl.pallas_call(
        smooth_kernel,
        out_shape=jax.ShapeDtypeStruct(obj.shape, F32),
        scratch_shapes=[pltpu.VMEM((2, rows + 16, width + 128), F32)],
        compiler_params=pltpu.CompilerParams(vmem_limit_bytes=40 * 2**20),
    )(obj, own, carried, above, below)


def gather_probes(probe):
    flat = probe.reshape(-1, HALF)
    count = lax.axis_size("pos")
    group = 32
    rows = flat.shape[0] // group
    mine = lax.axis_index("pos") % group
    piece = lax.dynamic_slice_in_dim(flat, mine * rows, rows, 0)
    piece = lax.all_gather(piece, "mode", axis=0)
    groups = [list(range(i, i + group)) for i in range(0, count, group)]
    pieces = lax.all_gather(piece, "pos", axis=1, axis_index_groups=groups)
    modes = lax.axis_size("mode")
    return pieces.reshape((modes,) + probe.shape[1:])


def per_device(object_field, probe, offsets, live, measured, gaps):
    stripe = object_field.shape[1]
    size = lax.axis_size("pos")
    here = lax.axis_index("pos")
    down = [(i, i + 1) for i in range(size - 1)]
    up = [(i + 1, i) for i in range(size - 1)]
    halo = lax.ppermute(object_field, "pos", up)
    probes = gather_probes(probe)
    rows = offsets[:, 0] - here * stripe
    spread = gradient(object_field, halo, probes, rows, offsets[:, 1], live, measured, gaps)
    last = object_field[:, stripe - 8 :] + UPDATE_RATE * spread[:, stripe - 8 : stripe]
    moved = lax.ppermute(jnp.concatenate([last, spread[:, stripe:]], 1), "pos", down)
    first = lax.ppermute(spread[:, :8], "pos", up)
    below = halo[:, :8] + UPDATE_RATE * (first + jnp.where(here < size - 1, spread[:, stripe : stripe + 8], 0.0))
    return smoothed(object_field, spread[:, :stripe], moved[:, 8:], moved[:, :8], below)


def solution(mesh):
    return jax.shard_map(
        per_device,
        mesh=mesh,
        in_specs=(
            P(None, "pos", None),
            P("mode", None, None, None),
            P("pos", None),
            P("pos"),
            P("pos", None, None),
            P(),
        ),
        out_specs=P(None, "pos", None),
        check_vma=False,
    )
```

time: 631 us -> 179 us (0.28)
  the two profiles are of different devices: /device:TPU:63 before, /device:TPU:64 now
where the time goes in v1:
time: 179 us
  waiting for transfers between devices  66.8 us (37%)
  starting transfers between devices  49 us (27%)
  blocking collectives  24.7 us (14%)
  Pallas kernels  15.3 us (9%)
  between operations  13.5 us (8%)
  local copies, waits for them, and re-layouts  7.11 us (4%)
  other arithmetic  2.18 us (1%)
    all_gather x1, waiting for transfers between devices, gather_probes(): pieces = lax.all_gather(piece, 'pos', axis=1, axis_index_groups=groups)  51 us
    ppermute x1, starting transfers between devices, per_device(): first = lax.ppermute(spread[:, :8], 'pos', up)  43 us
    all_gather x1, blocking collectives, gather_probes(): piece = lax.all_gather(piece, 'mode', axis=0)  24.7 us
    ppermute x1, waiting for transfers between devices, per_device(): lax.ppermute(jnp.concatenate([last, spread[:, stripe:]], 1), 'pos', down)  15.9 us
    pallas_call x1, Pallas kernels, gradient(): pl.pallas_call(grad_kernel, out_shape=jax.ShapeDtypeStruct((2, 2 * stripe...  13.7 us
    ppermute x1, starting transfers between devices, per_device(): halo = lax.ppermute(object_field, 'pos', up)  4.11 us
  transfers between devices with their start and end apart: 4, of which 2 were waited for; matrix products, arithmetic and copies ran while one was open for 3% of the time, Pallas kernels for 0%

profile of v1, /device:TPU:64, one launch (start us, length us, event | category | flops | bytes accessed | tf_op | source)
XLA Modules:
  0.0 178.6 jit_solution(4740383935622344417)
XLA Ops:
  6.5 0.0 all-gather.4.cloned.1.call-start
  6.5 1.1 reshape.8
  7.6 24.7 %all-gather = f32[128,128]{1,0:T(8,128)} all-gather(f32[32,128]{1,0:T(8,128)S(1)} %constant_dynamic-slice_fusion), channel_id=2, replica_groups=mesh['pos'=128,'mode'=4] {'mode'}, dimensions={0}, use_global_device_ids=true | all-gather | bytes 81920 | tf_op jit(solution)/shard_map/all_gather | solution.py:222
  32.4 0.0 all-gather.4.cloned.1.call-update
  32.4 4.1 %collective-permute-start = (f32[2,256,384]{2,1,0:T(8,128)}, f32[2,256,384]{2,1,0:T(8,128)S(1)}, u32[]{:S(2)}, u32[]{:S(2)}) collective-permute-start(f32[2,256,384]{2,1,0:T(8,128)} %obj.3), channel_id=1, source_target_pairs={{4,0},{8,4},{12,8},{16,12},{20,16},{24,20},{28,24},{32,28},{36,32}... | collective-permute-start | bytes 2359304 | tf_op jit(solution)/shard_map/ppermute | solution.py:235
  36.5 1.3 slice_bitcast_fusion
  37.9 51.0 %all-gather.4.cloned.1.call-done = f32[4,1024,128]{2,1,0:T(8,128)} async-done(((f32[4,32,128]{2,1,0:T(8,128)}), f32[4,1024,128]{2,1,0:T(8,128)}) %all-gather.4.cloned.1.call-update) | async-done | bytes 2097168 | tf_op jit(solution)/shard_map/all_gather | solution.py:224
  88.8 2.9 %reshape.9.probe = f32[4,2,256,256]{3,2,1,0:T(8,128)} reshape(f32[4,1024,128]{2,1,0:T(8,128)} %all-gather.4.cloned.1.call-done) | data formatting | bytes 4194304 | tf_op jit(solution)/shard_map/reshape | solution.py:226
  91.7 0.0 collective-permute-done.halo
  91.7 0.0 copy-start.1
  91.7 0.9 copy-done.1
  92.6 13.7 %shard_map.73 = f32[2,512,384]{2,1,0:T(8,128)} custom-call(s32[8]{0:T(128)} %get-tuple-element.10.rows, s32[8]{0:T(128)} %get-tuple-element.9.cols, s32[8]{0:T(128)} %live.1, f32[2,256,384]{2,1,0:T(8,128)} %obj.3, f32[2,256,384]{2,1,0:T(8,128)} %copy-done.1, f32[4,2,256,256]{3,2,1,0:T(8,128)} %reshape.9.probe, f32[8,256,256]{2,1,0:T(8,128)} %meas.1, ...), custom_call_target="tpu_custom_call" | custom-call | tf_op jit(solution)/shard_map/pallas_call | solution.py:157
  106.2 0.7 slice.50
  107.0 0.0 copy-start
  107.0 43.0 %collective-permute-start.2 = (f32[2,8,384]{2,1,0:T(8,128)S(1)}, f32[2,8,384]{2,1,0:T(8,128)S(1)}, u32[]{:S(2)}, u32[]{:S(2)}) collective-permute-start(f32[2,8,384]{2,1,0:T(8,128)S(1)} %slice.50), channel_id=1, source_target_pairs={{4,0},{8,4},{12,8},{16,12},{20,16},{24,20},{28,24},{32,28},{36,32}... | collective-permute-start | bytes 73736 | tf_op jit(solution)/shard_map/ppermute | solution.py:241
  149.9 1.5 fusion.4
  151.4 0.0 collective-permute-done.2
  151.5 0.0 copy-done
  151.5 0.8 fusion.2
  152.3 0.1 pad_maximum_fusion
  152.3 1.9 %collective-permute-start.1 = (f32[2,264,384]{2,1,0:T(8,128)S(1)}, f32[2,264,384]{2,1,0:T(8,128)S(1)}, u32[]{:S(2)}, u32[]{:S(2)}) collective-permute-start(f32[2,264,384]{2,1,0:T(8,128)S(1)} %pad_maximum_fusion), channel_id=1, source_target_pairs={{0,4},{4,8},{8,12},{12,16},{16,20},{20,24},{24,28},{28,32},{32,36}... | collective-permute-start | bytes 2433032 | tf_op jit(solution)/shard_map/ppermute | solution.py:240
  154.2 15.9 %collective-permute-done.1 = f32[2,264,384]{2,1,0:T(8,128)S(1)} collective-permute-done((f32[2,264,384]{2,1,0:T(8,128)S(1)}, f32[2,264,384]{2,1,0:T(8,128)S(1)}, u32[]{:S(2)}, u32[]{:S(2)}) %collective-permute-start.1) | collective-permute-done | bytes 811040 | tf_op jit(solution)/shard_map/ppermute | solution.py:240
  170.1 0.1 slice.47.carried
  170.2 1.6 shard_map.74
  (2 shorter events, 0.0 us)
Async XLA Ops:
  6.5 82.3 %all-gather.4.cloned.1.call-start = ((), (), s32[]{:S(2)}) async-start(), calls=%async_computation | async-start | bytes 2162688 | tf_op jit(solution)/shard_map/all_gather | solution.py:224
  32.4 59.3 %collective-permute-start = (f32[2,256,384]{2,1,0:T(8,128)}, f32[2,256,384]{2,1,0:T(8,128)S(1)}, u32[]{:S(2)}, u32[]{:S(2)}) collective-permute-start(f32[2,256,384]{2,1,0:T(8,128)} %obj.3), channel_id=1, source_target_pairs={{4,0},{8,4},{12,8},{16,12},{20,16},{24,20},{28,24},{32,28},{36,32}... | collective-permute-start | bytes 2359304 | tf_op jit(solution)/shard_map/ppermute | solution.py:235
  91.7 0.9 copy-start.1
  107.0 44.5 %copy-start = (f32[2,256,384]{2,1,0:T(8,128)S(1)}, f32[2,256,384]{2,1,0:T(8,128)}, u32[]{:S(2)}) copy-start(f32[2,256,384]{2,1,0:T(8,128)} %obj.3) | copy-start | bytes 2359300
  107.0 44.5 %collective-permute-start.2 = (f32[2,8,384]{2,1,0:T(8,128)S(1)}, f32[2,8,384]{2,1,0:T(8,128)S(1)}, u32[]{:S(2)}, u32[]{:S(2)}) collective-permute-start(f32[2,8,384]{2,1,0:T(8,128)S(1)} %slice.50), channel_id=1, source_target_pairs={{4,0},{8,4},{12,8},{16,12},{20,16},{24,20},{28,24},{32,28},{36,32}... | collective-permute-start | bytes 73736 | tf_op jit(solution)/shard_map/ppermute | solution.py:241
  152.3 17.8 %collective-permute-start.1 = (f32[2,264,384]{2,1,0:T(8,128)S(1)}, f32[2,264,384]{2,1,0:T(8,128)S(1)}, u32[]{:S(2)}, u32[]{:S(2)}) collective-permute-start(f32[2,264,384]{2,1,0:T(8,128)S(1)} %pad_maximum_fusion), channel_id=1, source_target_pairs={{0,4},{4,8},{8,12},{12,16},{16,20},{20,24},{24,28},{28,32},{32,36}... | collective-permute-start | bytes 2433032 | tf_op jit(solution)/shard_map/ppermute | solution.py:240
Sparse Core Ops, SparseCore 0:
  32.5 56.2 all-gather.3

commit v2 on v1

--- a/solution.py
+++ b/solution.py
@@ -12,6 +12,7 @@
 TALL = PATCH + 8
 F32 = jnp.float32
 BF16 = jnp.bfloat16
+MESH = pl.DeviceIdType.MESH
 UPDATE_RATE = 0.2
 SMOOTH_WEIGHT = 0.1
 GRADIENT_SOFTEN = 0.25
@@ -90,9 +91,9 @@
     return pick(0), pick(1)
 
 
-def grad_kernel(rows, cols, live, obj, halo, probe, meas, gaps, tab, acc, ext, spec, mask, scr):
+def grad_kernel(rows, cols, live, obj, halo, probe, others, meas, gaps, tab, acc, ext, spec, mask, scr):
     n = pl.program_id(0)
-    modes = probe.shape[0]
+    modes = spec.shape[0]
     width = obj.shape[2]
 
     @pl.when(n == 0)
@@ -122,11 +123,14 @@
             value = jnp.concatenate([value, jnp.zeros((TALL, width - PATCH), F32)], 1)
             acc[part, pl.ds(base, TALL), :] += pltpu.roll(value, col, 1)
 
+        def illumination(m):
+            return (probe[0, 0], probe[0, 1]) if m == 0 else (others[m - 1, 0], others[m - 1, 1])
+
         pr = cut(0)
         pi = cut(1)
         me = md = 0.0
         for m in range(modes):
-            br, bi = probe[m, 0], probe[m, 1]
+            br, bi = illumination(m)
             e, o = forward(br * pr - bi * pi, br * pi + bi * pr, tab)
             spec[m, 0] = e
             spec[m, 1] = o
@@ -142,14 +146,14 @@
         gr = gi = 0.0
         for m in range(modes):
             zr, zi = inverse(spec[m, 0] * re, spec[m, 1] * ro, tab)
-            br, bi = probe[m, 0], probe[m, 1]
+            br, bi = illumination(m)
             gr = gr + (br * zr + bi * zi)
             gi = gi + (br * zi - bi * zr)
         put(0, gr)
         put(1, gi)
 
 
-def gradient(obj, halo, probe, rows, cols, live, meas, gaps):
+def gradient(obj, halo, probe, others, rows, cols, live, meas, gaps):
     slots = meas.shape[0]
     stripe, width = obj.shape[1], obj.shape[2]
     tab = jnp.asarray(dft_tables())
@@ -164,6 +168,7 @@
                 whole(obj),
                 whole(halo),
                 whole(probe),
+                whole(others),
                 pl.BlockSpec((1, PATCH, PATCH), lambda n, *_: (n, 0, 0)),
                 whole(gaps),
                 whole(tab),
@@ -171,13 +176,13 @@
             out_specs=pl.BlockSpec((2, 2 * stripe, width), lambda n, *_: (0, 0, 0)),
             scratch_shapes=[
                 pltpu.VMEM((2, 2 * stripe, width), F32),
-                pltpu.VMEM((probe.shape[0], 2, PATCH, PATCH), F32),
+                pltpu.VMEM((1 + others.shape[0], 2, PATCH, PATCH), F32),
                 pltpu.VMEM((PATCH, PATCH), F32),
                 pltpu.VMEM((2, PATCH, HALF), F32),
             ],
         ),
         compiler_params=pltpu.CompilerParams(vmem_limit_bytes=56 * 2**20),
-    )(rows, cols, live, obj, halo, probe, meas, gaps, tab)
+    )(rows, cols, live, obj, halo, probe, others, meas, gaps, tab)
 
 
 def smooth_kernel(obj, own, carried, above, below, out, grid):
@@ -212,18 +217,89 @@
     )(obj, own, carried, above, below)
 
 
-def gather_probes(probe):
-    flat = probe.reshape(-1, HALF)
-    count = lax.axis_size("pos")
-    group = 32
-    rows = flat.shape[0] // group
-    mine = lax.axis_index("pos") % group
-    piece = lax.dynamic_slice_in_dim(flat, mine * rows, rows, 0)
-    piece = lax.all_gather(piece, "mode", axis=0)
-    groups = [list(range(i, i + group)) for i in range(0, count, group)]
-    pieces = lax.all_gather(piece, "pos", axis=1, axis_index_groups=groups)
+PLANE = 32
+CHIPS = 16
+
+
+def gather_kernel(probe, obj, others, halo, zs, zr, ps, pr, cs, cr, hs, hr):
+    me, mode = lax.axis_index("pos"), lax.axis_index("mode")
+    size, modes = lax.axis_size("pos"), lax.axis_size("mode")
+    lane = me % PLANE
+    plane, core, chip = me - lane, me % 2, lane // 2
+    sibling = me + 1 - 2 * core
+    before, after = (me + size - 1) % size, (me + 1) % size
+
+    def at(k):
+        return ((chip + k) % CHIPS) * 2 + core
+
+    barrier = pltpu.get_barrier_semaphore()
+    peers = [(me, (mode + d) % modes) for d in range(1, modes)]
+    peers += [(plane + at(k), mode) for k in range(1, CHIPS)]
+    peers += [(q, mode) for q in (sibling, before, after)]
+    for peer in peers:
+        pl.semaphore_signal(barrier, inc=1, device_id=peer, device_id_type=MESH)
+    pl.semaphore_wait(barrier, len(peers))
+
+    def send(src, dst, s, r, peer):
+        copy = pltpu.make_async_remote_copy(
+            src_ref=src, dst_ref=dst, send_sem=s, recv_sem=r, device_id=peer, device_id_type=MESH
+        )
+        copy.start()
+        return copy
+
+    across = [
+        send(probe.at[lane], others.at[modes - 1 - d, lane], zs.at[d - 1], zr.at[d - 1], (me, (mode + d) % modes))
+        for d in range(1, modes)
+    ]
+    edge = send(obj, halo, hs, hr, (before, mode))
+    for copy in across:
+        copy.wait_recv()
+
+    def block(k):
+        return others.at[:, at(k)]
+
+    spread = [
+        send(block(0), block(0), ps.at[k - 1], pr.at[k - 1], (plane + at(k), mode)) for k in range(1, CHIPS)
+    ]
+    twin = []
+    for k in range(CHIPS):
+        if k > 0:
+            spread[CHIPS - k - 1].wait_recv()
+        twin.append(send(block(k), block(k), cs.at[k], cr.at[k], (sibling, mode)))
+    for copy in twin:
+        copy.wait()
+    for copy in spread:
+        copy.wait_send()
+    for copy in across:
+        copy.wait_send()
+    edge.wait()
+
+
+def gather(probe, obj):
     modes = lax.axis_size("mode")
-    return pieces.reshape((modes,) + probe.shape[1:])
+    pieces = probe.reshape(PLANE, -1, PATCH)
+    dma = pltpu.SemaphoreType.DMA
+    others, halo = pl.pallas_call(
+        gather_kernel,
+        out_shape=(
+            jax.ShapeDtypeStruct((modes - 1,) + pieces.shape, F32),
+            jax.ShapeDtypeStruct(obj.shape, F32),
+        ),
+        in_specs=[pl.BlockSpec(memory_space=pl.ANY)] * 2,
+        out_specs=[pl.BlockSpec(memory_space=pl.ANY)] * 2,
+        scratch_shapes=[
+            dma((modes - 1,)),
+            dma((modes - 1,)),
+            dma((CHIPS - 1,)),
+            dma((CHIPS - 1,)),
+            dma((CHIPS,)),
+            dma((CHIPS,)),
+            dma,
+            dma,
+        ],
+        compiler_params=pltpu.CompilerParams(collective_id=0, has_side_effects=True),
+    )(pieces, obj)
+    return others.reshape((modes - 1,) + probe.shape[1:]), halo
 
 
 def per_device(object_field, probe, offsets, live, measured, gaps):
@@ -232,10 +308,10 @@
     here = lax.axis_index("pos")
     down = [(i, i + 1) for i in range(size - 1)]
     up = [(i + 1, i) for i in range(size - 1)]
-    halo = lax.ppermute(object_field, "pos", up)
-    probes = gather_probes(probe)
+    others, halo = gather(probe, object_field)
+    halo = jnp.where(here < size - 1, halo, 0.0)
     rows = offsets[:, 0] - here * stripe
-    spread = gradient(object_field, halo, probes, rows, offsets[:, 1], live, measured, gaps)
+    spread = gradient(object_field, halo, probe, others, rows, offsets[:, 1], live, measured, gaps)
     last = object_field[:, stripe - 8 :] + UPDATE_RATE * spread[:, stripe - 8 : stripe]
     moved = lax.ppermute(jnp.concatenate([last, spread[:, stripe:]], 1), "pos", down)
     first = lax.ppermute(spread[:, :8], "pos", up)

time: 179 us -> 119 us (0.66)
  the two profiles are of different devices: /device:TPU:64 before, /device:TPU:2 now
where the time goes in v2:
time: 119 us; the launch traced here: 118 us
  Pallas kernels  91.5 us (77%)
  waiting for transfers between devices  13.8 us (12%)
  starting transfers between devices  6.58 us (6%)
  other arithmetic  4.19 us (4%)
  local copies, waits for them, and re-layouts  2.29 us (2%)
    pallas_call x1, Pallas kernels, gradient(): pl.pallas_call(grad_kernel, out_shape=jax.ShapeDtypeStruct((2, 2 * stripe...  52.2 us
    pallas_call x1, Pallas kernels, gather(): pl.pallas_call(gather_kernel, out_shape=(jax.ShapeDtypeStruct((modes - 1,...  37.7 us
    ppermute x1, waiting for transfers between devices, per_device(): lax.ppermute(jnp.concatenate([last, spread[:, stripe:]], 1), 'pos', down)  13.8 us
    ppermute x1, starting transfers between devices, per_device(): first = lax.ppermute(spread[:, :8], 'pos', up)  4.66 us
  transfers between devices with their start and end apart: 2, of which 1 were waited for; matrix products, arithmetic and copies ran while one was open for 1% of the time, Pallas kernels for 0%

profile of v2, /device:TPU:2, one launch (start us, length us, event | category | flops | bytes accessed | tf_op | source)
XLA Modules:
  0.0 118.4 jit_solution(4480100876886370000)
XLA Ops:
  0.0 1.3 %slice_bitcast_fusion = (s32[8]{0:T(128)}, s32[8]{0:T(128)}) fusion(s32[8,2]{0,1:T(2,128)} %param.9, s32[]{:T(128)S(6)} %mul.9), kind=kLoop, calls=%fused_computation.8 | loop fusion | flops 8 | bytes 132 | tf_op jit(solution)/shard_map/squeeze | solution.py:314
  1.3 37.7 %shard_map.73 = (f32[3,32,16,256]{3,2,1,0:T(8,128)}, f32[2,256,384]{2,1,0:T(8,128)}) custom-call(f32[32,16,256]{2,1,0:T(8,128)} %bitcast.6, f32[2,256,384]{2,1,0:T(8,128)} %obj.5), custom_call_target="tpu_custom_call" | custom-call | tf_op jit(solution)/shard_map/pallas_call | solution.py:282
  39.0 2.1 %broadcast_select_fusion.halo = f32[2,256,384]{2,1,0:T(8,128)} fusion(f32[2,256,384]{2,1,0:T(8,128)} %get-tuple-element.7, pred[]{:T(512)S(6)} %lt.4), kind=kLoop, calls=%fused_computation.1 | loop fusion | flops 196608 | bytes 1572865 | tf_op jit(solution)/shard_map/jit(_where)/select_n | solution.py:312
  41.1 52.2 %shard_map.74 = f32[2,512,384]{2,1,0:T(8,128)} custom-call(s32[8]{0:T(128)} %get-tuple-element.14.rows, s32[8]{0:T(128)} %get-tuple-element.13.cols, s32[8]{0:T(128)} %live.1, f32[2,256,384]{2,1,0:T(8,128)} %obj.5, f32[2,256,384]{2,1,0:T(8,128)} %broadcast_select_fusion.halo, f32[1,2,256,256]{3,2,1,0:T(8,128)} %probe.1, f32[3,2,256,256]{3,2,1,0:T(8,128)} %bitcast.7, ...), custom_call_target="tpu_custom_call" | custom-call | tf_op jit(solution)/shard_map/pallas_call | solution.py:161
  93.2 0.7 slice.50
  94.0 0.0 copy-start
  94.0 4.7 %collective-permute-start.1 = (f32[2,8,384]{2,1,0:T(8,128)S(1)}, f32[2,8,384]{2,1,0:T(8,128)S(1)}, u32[]{:S(2)}, u32[]{:S(2)}) collective-permute-start(f32[2,8,384]{2,1,0:T(8,128)S(1)} %slice.50), channel_id=1, source_target_pairs={{4,0},{8,4},{12,8},{16,12},{20,16},{24,20},{28,24},{32,28},{36,32}... | collective-permute-start | bytes 73736 | tf_op jit(solution)/shard_map/ppermute | solution.py:317
  98.6 1.5 %fusion.4 = (f32[2,256,384]{2,1,0:T(8,128)S(1)}, f32[2,256,384]{2,1,0:T(8,128)S(1)}) fusion(f32[2,512,384]{2,1,0:T(8,128)} %shard_map.74), kind=kLoop, calls=%fused_computation.10 | loop fusion | bytes 3145728 | tf_op jit(solution)/shard_map/slice | solution.py:316
  100.1 0.0 collective-permute-done.1
  100.1 0.0 copy-done
  100.2 0.8 fusion.2
  101.0 0.1 pad_maximum_fusion
  101.0 1.9 %collective-permute-start = (f32[2,264,384]{2,1,0:T(8,128)S(1)}, f32[2,264,384]{2,1,0:T(8,128)S(1)}, u32[]{:S(2)}, u32[]{:S(2)}) collective-permute-start(f32[2,264,384]{2,1,0:T(8,128)S(1)} %pad_maximum_fusion), channel_id=1, source_target_pairs={{0,4},{4,8},{8,12},{12,16},{16,20},{20,24},{24,28},{28,32},{32,36}... | collective-permute-start | bytes 2433032 | tf_op jit(solution)/shard_map/ppermute | solution.py:316
  102.9 13.8 %collective-permute-done = f32[2,264,384]{2,1,0:T(8,128)S(1)} collective-permute-done((f32[2,264,384]{2,1,0:T(8,128)S(1)}, f32[2,264,384]{2,1,0:T(8,128)S(1)}, u32[]{:S(2)}, u32[]{:S(2)}) %collective-permute-start) | collective-permute-done | bytes 811040 | tf_op jit(solution)/shard_map/ppermute | solution.py:316
  116.7 0.1 slice.47.carried
  116.8 1.6 %shard_map.75 = f32[2,256,384]{2,1,0:T(8,128)} custom-call(f32[2,256,384]{2,1,0:T(8,128)S(1)} %copy-done, f32[2,256,384]{2,1,0:T(8,128)S(1)} %get-tuple-element.12.own, f32[2,256,384]{2,1,0:T(8,128)S(1)} %slice.47.carried, f32[2,8,384]{2,1,0:T(8,128)S(1)} %slice.48.above, f32[2,8,384]{2,1,0:T(8,128)S(1)} %get-tuple-element.9.below), custom_call_target="tpu_custom_call" | custom-call | tf_op jit(solution)/shard_map/pallas_call | solution.py:212
  (1 shorter events, 0.0 us)
Async XLA Ops:
  94.0 6.2 %copy-start = (f32[2,256,384]{2,1,0:T(8,128)S(1)}, f32[2,256,384]{2,1,0:T(8,128)}, u32[]{:S(2)}) copy-start(f32[2,256,384]{2,1,0:T(8,128)} %obj.5) | copy-start | bytes 2359300
  94.0 6.2 %collective-permute-start.1 = (f32[2,8,384]{2,1,0:T(8,128)S(1)}, f32[2,8,384]{2,1,0:T(8,128)S(1)}, u32[]{:S(2)}, u32[]{:S(2)}) collective-permute-start(f32[2,8,384]{2,1,0:T(8,128)S(1)} %slice.50), channel_id=1, source_target_pairs={{4,0},{8,4},{12,8},{16,12},{20,16},{24,20},{28,24},{32,28},{36,32}... | collective-permute-start | bytes 73736 | tf_op jit(solution)/shard_map/ppermute | solution.py:317
  101.0 15.7 %collective-permute-start = (f32[2,264,384]{2,1,0:T(8,128)S(1)}, f32[2,264,384]{2,1,0:T(8,128)S(1)}, u32[]{:S(2)}, u32[]{:S(2)}) collective-permute-start(f32[2,264,384]{2,1,0:T(8,128)S(1)} %pad_maximum_fusion), channel_id=1, source_target_pairs={{0,4},{4,8},{8,12},{12,16},{16,20},{20,24},{24,28},{28,32},{32,36}... | collective-permute-start | bytes 2433032 | tf_op jit(solution)/shard_map/ppermute | solution.py:316

commit v3 on v2

v3 whole, which is shorter than its diff:
```python
import jax
import jax.numpy as jnp
import ml_dtypes
import numpy as np
from jax import lax
from jax.experimental import pallas as pl
from jax.experimental.pallas import tpu as pltpu
from jax.sharding import PartitionSpec as P

PATCH = 256
HALF = PATCH // 2
LANES = 128
F32 = jnp.float32
BF16 = jnp.bfloat16
MESH = pl.DeviceIdType.MESH
UPDATE_RATE = 0.2
SMOOTH_WEIGHT = 0.1
GRADIENT_SOFTEN = 0.25


def dft_tables():
    k = np.arange(HALF)
    rows = []
    for odd in (0, 1):
        angle = 2.0 * np.pi * ((k[:, None] * (2 * k[None, :] + odd)) % PATCH) / PATCH
        c, s = np.cos(angle) / 16.0, np.sin(angle) / 16.0
        w = np.block([[c, -s], [s, c]])
        for m in (w, w.T):
            hi = m.astype(ml_dtypes.bfloat16)
            lo = (m - hi.astype(np.float64)).astype(ml_dtypes.bfloat16)
            rows += [hi, lo]
    order = np.concatenate([np.arange(0, PATCH, 2), np.arange(1, PATCH, 2)])
    shuffle = np.zeros((PATCH, PATCH), ml_dtypes.bfloat16)
    shuffle[order, np.arange(PATCH)] = 1
    rows.append(shuffle)
    return np.stack(rows)


def halves(x):
    hi = x.astype(BF16)
    return hi, (x - hi.astype(F32)).astype(BF16)


def dot(a, b):
    return jnp.dot(a, b, preferred_element_type=F32)


def product(a, b, c, d):
    return dot(a, c) + dot(a, d) + dot(b, c)


def right(x, tab, at):
    hi, lo = halves(x)
    return product(hi, lo, tab[at], tab[at + 1])


def left(tab, at, x):
    hi, lo = halves(x)
    return dot(tab[at], hi) + dot(tab[at + 1], hi) + dot(tab[at], lo)


WE, WET, WO, WOT, SHUF = 0, 2, 4, 6, 8


def fold(r, i):
    even = jnp.concatenate([r[:, :HALF] + r[:, HALF:], i[:, :HALF] + i[:, HALF:]], 1)
    odd = jnp.concatenate([r[:, :HALF] - r[:, HALF:], i[:, :HALF] - i[:, HALF:]], 1)
    return even, odd


def down_columns(e, o, tab):
    yr = jnp.concatenate([e[:, :HALF], o[:, :HALF]], 1)
    yi = jnp.concatenate([e[:, HALF:], o[:, HALF:]], 1)
    s = jnp.concatenate([yr[:HALF] + yr[HALF:], yi[:HALF] + yi[HALF:]], 0)
    d = jnp.concatenate([yr[:HALF] - yr[HALF:], yi[:HALF] - yi[HALF:]], 0)
    return left(tab, WET, s), left(tab, WOT, d)


def up_columns(te, to, tab):
    a, b = left(tab, WE, te), left(tab, WO, to)
    s, d = a + b, a - b
    zr = jnp.concatenate([s[:HALF], d[:HALF]], 0)
    zi = jnp.concatenate([s[HALF:], d[HALF:]], 0)
    return jnp.concatenate([zr[:, :HALF], zi[:, :HALF]], 1), jnp.concatenate([zr[:, HALF:], zi[:, HALF:]], 1)


def unzip_rows(x, scr):
    scr[0] = x[:, :HALF]
    scr[1] = x[:, HALF:]
    pick = lambda at: jnp.concatenate([scr[0, pl.ds(at, HALF, 2), :], scr[1, pl.ds(at, HALF, 2), :]], 1)
    return pick(0), pick(1)


def grad_kernel(
    offsets, live, obj, halo, probe, others, meas, gaps, tab,
    acc, ext, probes, counts, holes, wave, spec, ratio, mask, scr, sems,
):
    slots, stripe = meas.shape[0], obj.shape[1]
    modes = spec.shape[0]
    tiles = acc.shape[1]
    here = lax.axis_index("pos")
    lane = lax.broadcasted_iota(jnp.int32, (PATCH, LANES), 1)
    pairs = [(obj.at[:, :, LANES * t : LANES * (t + 1)], ext.at[:, t, :stripe]) for t in range(tiles)]
    pairs += [(halo.at[:, :, LANES * t : LANES * (t + 1)], ext.at[:, t, stripe:]) for t in range(tiles)]
    pairs += [(probe.at[0], probes.at[0]), (others, probes.at[1:])]
    pairs += [(tab, wave), (gaps, holes), (meas, counts)]
    copies = [pltpu.make_async_copy(src, dst, sems.at[k]) for k, (src, dst) in enumerate(pairs)]
    for copy in copies:
        copy.start()
    acc[...] = jnp.zeros_like(acc)
    total = live[0]
    for k in range(1, slots):
        total = total + live[k]
    for copy in copies:
        copy.wait()

    @pl.when(here == lax.axis_size("pos") - 1)
    def _():
        ext[:, :, stripe:] = jnp.zeros((2, tiles, stripe, LANES), F32)

    even, odd = unzip_rows(dot(holes[...].astype(F32).astype(BF16), wave[SHUF]), scr)
    mask[:HALF] = even
    mask[HALF:] = odd

    def place(n):
        return offsets[0, n] - here * stripe, offsets[1, n]

    def cut(n):
        row, col = place(n)
        back = lax.rem(LANES - col, LANES)
        near = lane < LANES - col
        parts = []
        for part in (0, 1):
            turned = [pltpu.roll(ext[part, t, pl.ds(row, PATCH), :], back, 1) for t in range(tiles)]
            parts.append(
                jnp.concatenate([jnp.where(near, turned[t], turned[t + 1]) for t in range(tiles - 1)], 1)
            )
        return parts

    def put(n, values):
        row, col = place(n)
        shift = lax.rem(col, LANES)
        inside = lane >= col
        for part, value in enumerate(values):
            turned = [pltpu.roll(value[:, LANES * t : LANES * (t + 1)], shift, 1) for t in range(tiles - 1)]
            for t in range(tiles):
                own = turned[t] if t < tiles - 1 else 0.0
                before = turned[t - 1] if t > 0 else 0.0
                acc[part, t, pl.ds(row, PATCH), :] += jnp.where(inside, own, before)

    def span(m):
        return slice(PATCH * m, PATCH * (m + 1))

    def forward(n):
        pr, pi = cut(n)
        folded = []
        for m in range(modes):
            br, bi = probes[m, 0], probes[m, 1]
            folded.append(fold(br * pr - bi * pi, br * pi + bi * pr))
        even = right(jnp.concatenate([x[0] for x in folded], 0), wave, WE)
        odd = right(jnp.concatenate([x[1] for x in folded], 0), wave, WO)
        me = md = 0.0
        for m in range(modes):
            e, o = down_columns(even[span(m)], odd[span(m)], wave)
            spec[m, 0] = e
            spec[m, 1] = o
            me = me + (e[:HALF] * e[:HALF] + e[HALF:] * e[HALF:])
            md = md + (o[:HALF] * o[:HALF] + o[HALF:] * o[HALF:])
        hi, lo = halves(jnp.sqrt(counts[n]))
        even, odd = unzip_rows(dot(hi, wave[SHUF]) + dot(lo, wave[SHUF]), scr)
        ratio[:HALF] = mask[:HALF] * (even * lax.rsqrt(jnp.maximum(me, 0.0625)) - 1.0)
        ratio[HALF:] = mask[HALF:] * (odd * lax.rsqrt(jnp.maximum(md, 0.0625)) - 1.0)

    def inverse(n):
        re, ro = ratio[:HALF], ratio[HALF:]
        re = jnp.concatenate([re, re], 0)
        ro = jnp.concatenate([ro, ro], 0)
        z = [up_columns(spec[m, 0] * re, spec[m, 1] * ro, wave) for m in range(modes)]
        a = right(jnp.concatenate([x[0] for x in z], 0), wave, WET)
        b = right(jnp.concatenate([x[1] for x in z], 0), wave, WOT)
        gr = gi = 0.0
        for m in range(modes):
            s, d = a[span(m)] + b[span(m)], a[span(m)] - b[span(m)]
            zr = jnp.concatenate([s[:, :HALF], d[:, :HALF]], 1)
            zi = jnp.concatenate([s[:, HALF:], d[:, HALF:]], 1)
            br, bi = probes[m, 0], probes[m, 1]
            gr = gr + (br * zr + bi * zi)
            gi = gi + (br * zi - bi * zr)
        put(n, (gr, gi))

    def visit(n, carry):
        inverse(n)
        forward(n + 1)
        return carry

    forward(0)
    lax.fori_loop(0, total - 1, visit, 0)
    inverse(total - 1)


def gradient(obj, halo, probe, others, offsets, live, meas, gaps):
    stripe, width = obj.shape[1:]
    modes = 1 + others.shape[0]
    tiles = width // LANES
    tab = jnp.asarray(dft_tables())
    smem, hbm = pl.BlockSpec(memory_space=pltpu.SMEM), pl.BlockSpec(memory_space=pl.ANY)
    return pl.pallas_call(
        grad_kernel,
        out_shape=jax.ShapeDtypeStruct((2, tiles, 2 * stripe, LANES), F32),
        in_specs=[smem] * 2 + [hbm] * 7,
        out_specs=pl.BlockSpec(memory_space=pltpu.VMEM),
        scratch_shapes=[
            pltpu.VMEM((2, tiles, 2 * stripe, LANES), F32),
            pltpu.VMEM((modes, 2, PATCH, PATCH), F32),
            pltpu.VMEM(meas.shape, F32),
            pltpu.VMEM(gaps.shape, jnp.int32),
            pltpu.VMEM(tab.shape, BF16),
            pltpu.VMEM((modes, 2, PATCH, PATCH), F32),
            pltpu.VMEM((PATCH, PATCH), F32),
            pltpu.VMEM((PATCH, PATCH), F32),
            pltpu.VMEM((2, PATCH, HALF), F32),
            pltpu.SemaphoreType.DMA((2 * tiles + 5,)),
        ],
        compiler_params=pltpu.CompilerParams(vmem_limit_bytes=56 * 2**20),
    )(offsets.T, live, obj, halo, probe, others, meas, gaps, tab)


PLANE = 32
CHIPS = 16


def gather_kernel(probe, obj, others, halo, zs, zr, ps, pr, cs, cr, hs, hr):
    me, mode = lax.axis_index("pos"), lax.axis_index("mode")
    size, modes = lax.axis_size("pos"), lax.axis_size("mode")
    lane = me % PLANE
    plane, core, chip = me - lane, me % 2, lane // 2
    sibling = me + 1 - 2 * core
    before, after = (me + size - 1) % size, (me + 1) % size

    def at(k):
        return ((chip + k) % CHIPS) * 2 + core

    barrier = pltpu.get_barrier_semaphore()
    peers = [(me, (mode + d) % modes) for d in range(1, modes)]
    peers += [(plane + at(k), mode) for k in range(1, CHIPS)]
    peers += [(q, mode) for q in (sibling, before, after)]
    for peer in peers:
        pl.semaphore_signal(barrier, inc=1, device_id=peer, device_id_type=MESH)
    pl.semaphore_wait(barrier, len(peers))

    def send(src, dst, s, r, peer):
        copy = pltpu.make_async_remote_copy(
            src_ref=src, dst_ref=dst, send_sem=s, recv_sem=r, device_id=peer, device_id_type=MESH
        )
        copy.start()
        return copy

    across = [
        send(probe.at[lane], others.at[modes - 1 - d, lane], zs.at[d - 1], zr.at[d - 1], (me, (mode + d) % modes))
        for d in range(1, modes)
    ]
    edge = send(obj, halo, hs, hr, (before, mode))
    for copy in across:
        copy.wait_recv()

    def block(k):
        return others.at[:, at(k)]

    spread = [
        send(block(0), block(0), ps.at[k - 1], pr.at[k - 1], (plane + at(k), mode)) for k in range(1, CHIPS)
    ]
    twin = []
    for k in range(CHIPS):
        if k > 0:
            spread[CHIPS - k - 1].wait_recv()
        twin.append(send(block(k), block(k), cs.at[k], cr.at[k], (sibling, mode)))
    for copy in twin:
        copy.wait()
    for copy in spread:
        copy.wait_send()
    for copy in across:
        copy.wait_send()
    edge.wait()


def gather(probe, obj):
    modes = lax.axis_size("mode")
    pieces = probe.reshape(PLANE, -1, PATCH)
    dma = pltpu.SemaphoreType.DMA
    others, halo = pl.pallas_call(
        gather_kernel,
        out_shape=(
            jax.ShapeDtypeStruct((modes - 1,) + pieces.shape, F32),
            jax.ShapeDtypeStruct(obj.shape, F32),
        ),
        in_specs=[pl.BlockSpec(memory_space=pl.ANY)] * 2,
        out_specs=[pl.BlockSpec(memory_space=pl.ANY)] * 2,
        scratch_shapes=[
            dma((modes - 1,)),
            dma((modes - 1,)),
            dma((CHIPS - 1,)),
            dma((CHIPS - 1,)),
            dma((CHIPS,)),
            dma((CHIPS,)),
            dma,
            dma,
        ],
        compiler_params=pltpu.CompilerParams(collective_id=0, has_side_effects=True),
    )(pieces, obj)
    return others.reshape((modes - 1,) + probe.shape[1:]), halo


def tail_kernel(spread, obj, halo, out, grid, field, own, edge, landed, before, first, locals_, ss, rs):
    me, mode = lax.axis_index("pos"), lax.axis_index("mode")
    size = lax.axis_size("pos")
    rows, width = obj.shape[1:]
    previous, following = (me + size - 1) % size, (me + 1) % size
    barrier = pltpu.get_barrier_semaphore()
    for q in (previous, following):
        pl.semaphore_signal(barrier, inc=1, device_id=(q, mode), device_id_type=MESH)
    near = [
        pltpu.make_async_copy(src, dst, locals_.at[k])
        for k, (src, dst) in enumerate([(obj, field), (spread.at[:, :, : rows + 8], own), (halo.at[:, :8], edge)])
    ]
    for copy in near:
        copy.start()
    pl.semaphore_wait(barrier, 2)
    far = [
        (spread.at[:, :, rows - 8 :], landed, following),
        (obj.at[:, rows - 8 :], before, following),
        (spread.at[:, :, :8], first, previous),
    ]
    far = [
        pltpu.make_async_remote_copy(
            src_ref=src, dst_ref=dst, send_sem=ss.at[k], recv_sem=rs.at[k], device_id=(q, mode), device_id_type=MESH
        )
        for k, (src, dst, q) in enumerate(far)
    ]
    for copy in far:
        copy.start()
    for copy in near:
        copy.wait()
    grid[...] = jnp.zeros_like(grid)
    for copy in far:
        copy.wait()
    top = jnp.where(me > 0, 1.0, 0.0)
    bottom = jnp.where(me < size - 1, 1.0, 0.0)
    for k in range(width // LANES):
        at = slice(LANES * k, LANES * (k + 1))
        grid[:, 0:8, at] = top * (before[:, :, at] + UPDATE_RATE * landed[:, k, :8])
        grid[:, 8 : rows + 8, at] = field[:, :, at] + UPDATE_RATE * (own[:, k, :rows] + top * landed[:, k, 8:])
        grid[:, rows + 8 :, at] = bottom * (edge[:, :, at] + UPDATE_RATE * (first[:, k] + own[:, k, rows:]))
    total = GRADIENT_SOFTEN
    pairs = []
    for part in (0, 1):
        u = grid[part]
        drow = pltpu.roll(u, u.shape[0] - 1, 0) - u
        dcol = pltpu.roll(u, u.shape[1] - 1, 1) - u
        total = total + drow * drow + dcol * dcol
        pairs.append((u, drow, dcol))
    inv = lax.rsqrt(total)
    for part, (u, drow, dcol) in enumerate(pairs):
        vrow, vcol = drow * inv, dcol * inv
        change = vrow - pltpu.roll(vrow, 1, 0) + vcol - pltpu.roll(vcol, 1, 1)
        out[part] = (u + SMOOTH_WEIGHT * change)[8 : rows + 8, :width]


def finish(spread, obj, halo):
    rows, width = obj.shape[1:]
    tiles = width // LANES
    hbm, dma = pl.BlockSpec(memory_space=pl.ANY), pltpu.SemaphoreType.DMA
    return pl.pallas_call(
        tail_kernel,
        out_shape=jax.ShapeDtypeStruct(obj.shape, F32),
        in_specs=[hbm] * 3,
        out_specs=pl.BlockSpec(memory_space=pltpu.VMEM),
        scratch_shapes=[
            pltpu.VMEM((2, rows + 16, width + 128), F32),
            pltpu.VMEM((2, rows, width), F32),
            pltpu.VMEM((2, tiles, rows + 8, LANES), F32),
            pltpu.VMEM((2, 8, width), F32),
            pltpu.VMEM((2, tiles, rows + 8, LANES), F32),
            pltpu.VMEM((2, 8, width), F32),
            pltpu.VMEM((2, tiles, 8, LANES), F32),
            dma((3,)),
            dma((3,)),
            dma((3,)),
        ],
        compiler_params=pltpu.CompilerParams(collective_id=1, has_side_effects=True, vmem_limit_bytes=56 * 2**20),
    )(spread, obj, halo)


def per_device(object_field, probe, offsets, live, measured, gaps):
    others, halo = gather(probe, object_field)
    spread = gradient(object_field, halo, probe, others, offsets, live, measured, gaps)
    return finish(spread, object_field, halo)


def solution(mesh):
    return jax.shard_map(
        per_device,
        mesh=mesh,
        in_specs=(
            P(None, "pos", None),
            P("mode", None, None, None),
            P("pos", None),
            P("pos"),
            P("pos", None, None),
            P(),
        ),
        out_specs=P(None, "pos", None),
        check_vma=False,
    )
```

time: 119 us -> 98.6 us (0.83)
  the two profiles are of different devices: /device:TPU:2 before, /device:TPU:64 now
where the time goes in v3:
time: 98.6 us; the launch traced here: 98.4 us
  Pallas kernels  96.3 us (98%)
  local copies, waits for them, and re-layouts  2.06 us (2%)
    pallas_call x1, Pallas kernels, finish(): pl.pallas_call(tail_kernel, out_shape=jax.ShapeDtypeStruct(obj.shape, F32...  41.9 us
    pallas_call x1, Pallas kernels, gather(): pl.pallas_call(gather_kernel, out_shape=(jax.ShapeDtypeStruct((modes - 1,...  35.9 us
    pallas_call x1, Pallas kernels, gradient(): pl.pallas_call(grad_kernel, out_shape=jax.ShapeDtypeStruct((2, tiles, 2 *...  18.5 us
    unnamed x1, local copies, waits for them, and re-layouts  2.06 us

profile of v3, /device:TPU:64, one launch (start us, length us, event | category | flops | bytes accessed | tf_op | source)
XLA Modules:
  0.0 98.4 jit_solution(17203622477065202694)
XLA Ops:
  0.0 35.9 %shard_map.73 = (f32[3,32,16,256]{3,2,1,0:T(8,128)}, f32[2,256,384]{2,1,0:T(8,128)}) custom-call(f32[32,16,256]{2,1,0:T(8,128)} %bitcast.3, f32[2,256,384]{2,1,0:T(8,128)} %obj.5), custom_call_target="tpu_custom_call" | custom-call | tf_op jit(solution)/shard_map/pallas_call | solution.py:290
  35.9 18.5 %shard_map.74.spread = f32[2,3,512,128]{3,2,1,0:T(8,128)} custom-call(s32[2,8]{1,0:T(2,128)} %bitcast.5, s32[8]{0:T(128)} %live.1, f32[2,256,384]{2,1,0:T(8,128)} %obj.5, f32[2,256,384]{2,1,0:T(8,128)} %get-tuple-element.7.halo, f32[1,2,256,256]{3,2,1,0:T(8,128)} %probe.1, f32[3,2,256,256]{3,2,1,0:T(8,128)} %bitcast.4, f32[8,256,256]{2,1,0:T(8,128)} %meas.1, ...), custom_call_target="tpu_custom_call" | custom-call | tf_op jit(solution)/shard_map/pallas_call | solution.py:207
  54.4 41.9 %shard_map.75 = f32[2,256,384]{2,1,0:T(8,128)} custom-call(f32[2,3,512,128]{3,2,1,0:T(8,128)} %shard_map.74.spread, f32[2,256,384]{2,1,0:T(8,128)} %obj.5, f32[2,256,384]{2,1,0:T(8,128)} %get-tuple-element.7.halo), custom_call_target="tpu_custom_call" | custom-call | tf_op jit(solution)/shard_map/pallas_call | solution.py:372
  96.3 2.1 %copy.9 = f32[2,256,384]{2,1,0:T(8,128)} copy(f32[2,256,384]{2,1,0:T(8,128)} %shard_map.75) | data formatting | bytes 1572864

commit v4 on v3

v4 whole, which is shorter than its diff:
```python
import jax
import jax.numpy as jnp
import ml_dtypes
import numpy as np
from jax import lax
from jax.experimental import pallas as pl
from jax.experimental.pallas import tpu as pltpu
from jax.sharding import PartitionSpec as P

PATCH = 256
HALF = PATCH // 2
LANES = 128
F32 = jnp.float32
BF16 = jnp.bfloat16
MESH = pl.DeviceIdType.MESH
UPDATE_RATE = 0.2
SMOOTH_WEIGHT = 0.1
GRADIENT_SOFTEN = 0.25


def dft_tables():
    k = np.arange(HALF)
    rows = []
    for odd in (0, 1):
        angle = 2.0 * np.pi * ((k[:, None] * (2 * k[None, :] + odd)) % PATCH) / PATCH
        c, s = np.cos(angle) / 16.0, np.sin(angle) / 16.0
        w = np.block([[c, -s], [s, c]])
        for m in (w, w.T):
            hi = m.astype(ml_dtypes.bfloat16)
            lo = (m - hi.astype(np.float64)).astype(ml_dtypes.bfloat16)
            rows += [hi, lo]
    order = np.concatenate([np.arange(0, PATCH, 2), np.arange(1, PATCH, 2)])
    shuffle = np.zeros((PATCH, PATCH), ml_dtypes.bfloat16)
    shuffle[order, np.arange(PATCH)] = 1
    rows.append(shuffle)
    return np.stack(rows)


def halves(x):
    hi = x.astype(BF16)
    return hi, (x - hi.astype(F32)).astype(BF16)


def dot(a, b):
    return jnp.dot(a, b, preferred_element_type=F32)


def product(a, b, c, d):
    return dot(a, c) + dot(a, d) + dot(b, c)


def right(x, tab, at):
    hi, lo = halves(x)
    return product(hi, lo, tab[at], tab[at + 1])


def left(tab, at, x):
    hi, lo = halves(x)
    return dot(tab[at], hi) + dot(tab[at + 1], hi) + dot(tab[at], lo)


WE, WET, WO, WOT, SHUF = 0, 2, 4, 6, 8


def fold(r, i):
    even = jnp.concatenate([r[:, :HALF] + r[:, HALF:], i[:, :HALF] + i[:, HALF:]], 1)
    odd = jnp.concatenate([r[:, :HALF] - r[:, HALF:], i[:, :HALF] - i[:, HALF:]], 1)
    return even, odd


def down_columns(e, o, tab):
    yr = jnp.concatenate([e[:, :HALF], o[:, :HALF]], 1)
    yi = jnp.concatenate([e[:, HALF:], o[:, HALF:]], 1)
    s = jnp.concatenate([yr[:HALF] + yr[HALF:], yi[:HALF] + yi[HALF:]], 0)
    d = jnp.concatenate([yr[:HALF] - yr[HALF:], yi[:HALF] - yi[HALF:]], 0)
    return left(tab, WET, s), left(tab, WOT, d)


def up_columns(te, to, tab):
    a, b = left(tab, WE, te), left(tab, WO, to)
    s, d = a + b, a - b
    zr = jnp.concatenate([s[:HALF], d[:HALF]], 0)
    zi = jnp.concatenate([s[HALF:], d[HALF:]], 0)
    return jnp.concatenate([zr[:, :HALF], zi[:, :HALF]], 1), jnp.concatenate([zr[:, HALF:], zi[:, HALF:]], 1)


def unzip_rows(x, scr):
    scr[0] = x[:, :HALF]
    scr[1] = x[:, HALF:]
    pick = lambda at: jnp.concatenate([scr[0, pl.ds(at, HALF, 2), :], scr[1, pl.ds(at, HALF, 2), :]], 1)
    return pick(0), pick(1)


PLANE = 32
CHIPS = 16
BATCH = 4


def fused_kernel(
    offsets, live, obj, probe, meas, gaps, tab,
    out, acc, ext, probes, counts, holes, wave, patches, first, spec, ratio, mask, scr, wide,
    sems, zs, zr, ps, pr, cs, cr, hs, hr,
):
    slots, stripe = meas.shape[0], obj.shape[1]
    modes = probes.shape[0]
    tiles = ext.shape[1]
    me, mode = lax.axis_index("pos"), lax.axis_index("mode")
    size = lax.axis_size("pos")
    lane_of = me % PLANE
    plane, core, chip = me - lane_of, me % 2, lane_of // 2
    sibling = me + 1 - 2 * core
    before, after = (me + size - 1) % size, (me + 1) % size
    lane = lax.broadcasted_iota(jnp.int32, (PATCH, LANES), 1)

    def cols(t):
        return slice(LANES * t, LANES * (t + 1))

    pairs = [(tab, wave), (meas, counts), (gaps, holes), (probe, probes.at[0])]
    pairs += [(obj.at[:, :, cols(t)], ext.at[:, t, :stripe]) for t in range(tiles)]
    copies = [pltpu.make_async_copy(src, dst, sems.at[k]) for k, (src, dst) in enumerate(pairs)]
    for copy in copies:
        copy.start()

    def at(k):
        return ((chip + k) % CHIPS) * 2 + core

    barrier = pltpu.get_barrier_semaphore()
    peers = [(me, (mode + d) % modes) for d in range(1, modes)]
    peers += [(plane + at(k), mode) for k in range(1, CHIPS)]
    peers += [(q, mode) for q in (sibling, before, after)]
    for peer in peers:
        pl.semaphore_signal(barrier, inc=1, device_id=peer, device_id_type=MESH)
    pl.semaphore_wait(barrier, len(peers))

    def send(src, dst, s, r, peer):
        copy = pltpu.make_async_remote_copy(
            src_ref=src, dst_ref=dst, send_sem=s, recv_sem=r, device_id=peer, device_id_type=MESH
        )
        copy.start()
        return copy

    across = [
        send(probe.at[lane_of], probes.at[modes - d, lane_of], zs.at[d - 1], zr.at[d - 1], (me, (mode + d) % modes))
        for d in range(1, modes)
    ]
    edge = [
        send(obj.at[:, :, cols(t)], ext.at[:, t, stripe:], hs.at[t], hr.at[t], (before, mode)) for t in range(tiles)
    ]

    acc[...] = jnp.zeros_like(acc)
    wide[...] = jnp.zeros_like(wide)
    for copy in copies:
        copy.wait()
    even, odd = unzip_rows(dot(holes[...].astype(F32).astype(BF16), wave[SHUF]), scr)
    mask[:HALF] = even
    mask[HALF:] = odd

    def unzip(n, carry):
        hi, lo = halves(jnp.sqrt(counts[n]))
        even, odd = unzip_rows(dot(hi, wave[SHUF]) + dot(lo, wave[SHUF]), scr)
        counts[n, :HALF] = even
        counts[n, HALF:] = odd
        return carry

    lax.fori_loop(0, slots, unzip, 0)

    for copy in across:
        copy.wait_recv()

    def block(k):
        return probes.at[pl.ds(1, modes - 1), at(k)]

    spread = [
        send(block(0), block(0), ps.at[k - 1], pr.at[k - 1], (plane + at(k), mode)) for k in range(1, CHIPS)
    ]
    twin = [send(block(0), block(0), cs.at[0], cr.at[0], (sibling, mode))]
    for copy in edge:
        copy.wait_recv()

    @pl.when(me == size - 1)
    def _():
        ext[:, :, stripe:] = jnp.zeros((2, tiles, stripe, LANES), F32)

    def place(n):
        return lax.rem(offsets[0, n], stripe), offsets[1, n]

    def cut(n):
        row, col = place(n)
        back = lax.rem(LANES - col, LANES)
        near = lane < LANES - col
        parts = []
        for part in (0, 1):
            turned = [pltpu.roll(ext[part, t, pl.ds(row, PATCH), :], back, 1) for t in range(tiles)]
            parts.append(
                jnp.concatenate([jnp.where(near, turned[t], turned[t + 1]) for t in range(tiles - 1)], 1)
            )
        return parts

    def put(n, values):
        row, col = place(n)
        shift = lax.rem(col, LANES)
        inside = lane >= col
        for part, value in enumerate(values):
            turned = [pltpu.roll(value[:, cols(t)], shift, 1) for t in range(tiles - 1)]
            for t in range(tiles):
                own = turned[t] if t < tiles - 1 else 0.0
                left_of = turned[t - 1] if t > 0 else 0.0
                wide[part, t, stripe : stripe + PATCH] = jnp.where(inside, own, left_of)
                acc[part * tiles + t] += wide[part, t, pl.ds(stripe - row, 2 * stripe), :]

    def span(m):
        return slice(PATCH * m, PATCH * (m + 1))

    def light(m):
        half = PLANE // 2
        return probes[m, :half].reshape(PATCH, PATCH), probes[m, half:].reshape(PATCH, PATCH)

    def transformed(items):
        folded = []
        for m, (xr, xi) in items:
            br, bi = light(m)
            folded.append(fold(br * xr - bi * xi, br * xi + bi * xr))
        even = right(jnp.concatenate([x[0] for x in folded], 0), wave, WE)
        odd = right(jnp.concatenate([x[1] for x in folded], 0), wave, WO)
        return [down_columns(even[span(k)], odd[span(k)], wave) for k in range(len(folded))]

    def own(g, carry):
        taken = []
        for k in range(BATCH):
            n = g * BATCH + k
            xr, xi = cut(n)
            patches[n, 0] = xr
            patches[n, 1] = xi
            taken.append((0, (xr, xi)))
        for k, (e, o) in enumerate(transformed(taken)):
            first[g * BATCH + k, 0] = e
            first[g * BATCH + k, 1] = o
        return carry

    lax.fori_loop(0, slots // BATCH, own, 0)

    for k in range(1, CHIPS):
        spread[CHIPS - k - 1].wait_recv()
        twin.append(send(block(k), block(k), cs.at[k], cr.at[k], (sibling, mode)))
    for copy in twin:
        copy.wait_recv()

    def power(x):
        return x[:HALF] * x[:HALF] + x[HALF:] * x[HALF:]

    def forward(n):
        patch = patches[n, 0], patches[n, 1]
        me_, mo_ = power(first[n, 0]), power(first[n, 1])
        for k, (e, o) in enumerate(transformed([(m, patch) for m in range(1, modes)])):
            spec[k, 0] = e
            spec[k, 1] = o
            me_ = me_ + power(e)
            mo_ = mo_ + power(o)
        alive = jnp.where(live[n] > 0, 1.0, 0.0)
        for at_, total in ((slice(0, HALF), me_), (slice(HALF, PATCH), mo_)):
            change = counts[n, at_] * lax.rsqrt(jnp.maximum(total, 0.0625)) - 1.0
            ratio[at_] = (alive * mask[at_]) * change

    def inverse(n):
        re, ro = ratio[:HALF], ratio[HALF:]
        re = jnp.concatenate([re, re], 0)
        ro = jnp.concatenate([ro, ro], 0)
        source = [(first[n, 0], first[n, 1])] + [(spec[k, 0], spec[k, 1]) for k in range(modes - 1)]
        z = [up_columns(e * re, o * ro, wave) for e, o in source]
        a = right(jnp.concatenate([x[0] for x in z], 0), wave, WET)
        b = right(jnp.concatenate([x[1] for x in z], 0), wave, WOT)
        gr = gi = 0.0
        for m in range(modes):
            s, d = a[span(m)] + b[span(m)], a[span(m)] - b[span(m)]
            zr = jnp.concatenate([s[:, :HALF], d[:, :HALF]], 1)
            zi = jnp.concatenate([s[:, HALF:], d[:, HALF:]], 1)
            br, bi = light(m)
            gr = gr + (br * zr + bi * zi)
            gi = gi + (br * zi - bi * zr)
        put(n, (gr, gi))

    def visit(n, carry):
        inverse(n)
        forward(n + 1)
        return carry

    forward(0)
    lax.fori_loop(0, slots - 1, visit, 0)
    inverse(slots - 1)
    done = pltpu.make_async_copy(acc, out, sems.at[0])
    done.start()
    for copy in across + edge + spread + twin:
        copy.wait_send()
    done.wait()


def gradient(obj, probe, offsets, live, meas, gaps):
    stripe, width = obj.shape[1:]
    modes = lax.axis_size("mode")
    slots = meas.shape[0]
    tiles = width // LANES
    tab = jnp.asarray(dft_tables())
    pieces = probe.reshape(PLANE, -1, PATCH)
    smem, hbm = pl.BlockSpec(memory_space=pltpu.SMEM), pl.BlockSpec(memory_space=pl.ANY)
    vmem, dma = pltpu.VMEM, pltpu.SemaphoreType.DMA
    spread = pl.pallas_call(
        fused_kernel,
        out_shape=jax.ShapeDtypeStruct((2 * tiles, 2 * stripe, LANES), F32),
        in_specs=[smem] * 2 + [hbm] * 5,
        out_specs=hbm,
        scratch_shapes=[
            vmem((2 * tiles, 2 * stripe, LANES), F32),
            vmem((2, tiles, 2 * stripe, LANES), F32),
            vmem((modes,) + pieces.shape, F32),
            vmem(meas.shape, F32),
            vmem(gaps.shape, jnp.int32),
            vmem(tab.shape, BF16),
            vmem((slots, 2, PATCH, PATCH), F32),
            vmem((slots, 2, PATCH, PATCH), F32),
            vmem((modes - 1, 2, PATCH, PATCH), F32),
            vmem((PATCH, PATCH), F32),
            vmem((PATCH, PATCH), F32),
            vmem((2, PATCH, HALF), F32),
            vmem((2, tiles, 3 * stripe, LANES), F32),
            dma((4 + tiles,)),
            dma((modes - 1,)),
            dma((modes - 1,)),
            dma((CHIPS - 1,)),
            dma((CHIPS - 1,)),
            dma((CHIPS,)),
            dma((CHIPS,)),
            dma((tiles,)),
            dma((tiles,)),
        ],
        compiler_params=pltpu.CompilerParams(
            collective_id=0, has_side_effects=True, vmem_limit_bytes=60 * 2**20
        ),
    )(offsets.T, live, obj, pieces, meas, gaps, tab)
    return spread.reshape(2, tiles, 2 * stripe, LANES)


def tail_kernel(spread, obj, landed, before, first, beyond, ss, rs):
    me, mode = lax.axis_index("pos"), lax.axis_index("mode")
    size, rows = lax.axis_size("pos"), obj.shape[1]
    previous, following = (me + size - 1) % size, (me + 1) % size
    barrier = pltpu.get_barrier_semaphore()
    for q in (previous, following):
        pl.semaphore_signal(barrier, inc=1, device_id=(q, mode), device_id_type=MESH)
    pl.semaphore_wait(barrier, 2)
    far = [
        (spread.at[:, :, rows - 8 :], landed, following),
        (obj.at[:, rows - 8 :], before, following),
        (spread.at[:, :, :8], first, previous),
        (obj.at[:, :8], beyond, previous),
    ]
    far = [
        pltpu.make_async_remote_copy(
            src_ref=src, dst_ref=dst, send_sem=ss.at[k], recv_sem=rs.at[k], device_id=(q, mode), device_id_type=MESH
        )
        for k, (src, dst, q) in enumerate(far)
    ]
    for copy in far:
        copy.start()
    for copy in far:
        copy.wait()


def exchange(spread, obj):
    rows, width = obj.shape[1:]
    tiles = width // LANES
    hbm, dma = pl.BlockSpec(memory_space=pl.ANY), pltpu.SemaphoreType.DMA
    return pl.pallas_call(
        tail_kernel,
        out_shape=(
            jax.ShapeDtypeStruct((2, tiles, rows + 8, LANES), F32),
            jax.ShapeDtypeStruct((2, 8, width), F32),
            jax.ShapeDtypeStruct((2, tiles, 8, LANES), F32),
            jax.ShapeDtypeStruct((2, 8, width), F32),
        ),
        in_specs=[hbm] * 2,
        out_specs=[hbm] * 4,
        scratch_shapes=[dma((4,)), dma((4,))],
        compiler_params=pltpu.CompilerParams(collective_id=1, has_side_effects=True),
    )(spread, obj)


def smooth_kernel(spread, obj, beyond, landed_, before_, first_, out, grid, field, own, edge, landed, before, first, sems):
    rows, width = obj.shape[1:]
    me, size = lax.axis_index("pos"), lax.axis_size("pos")
    near = [
        (landed_, landed), (spread.at[:, :, : rows + 8], own), (obj, field),
        (beyond, edge), (before_, before), (first_, first),
    ]
    near = [pltpu.make_async_copy(src, dst, sems.at[k]) for k, (src, dst) in enumerate(near)]
    for copy in near:
        copy.start()
    grid[...] = jnp.zeros_like(grid)
    for copy in near:
        copy.wait()
    top = jnp.where(me > 0, 1.0, 0.0)
    bottom = jnp.where(me < size - 1, 1.0, 0.0)
    for k in range(width // LANES):
        at = slice(LANES * k, LANES * (k + 1))
        grid[:, 0:8, at] = top * (before[:, :, at] + UPDATE_RATE * landed[:, k, :8])
        grid[:, 8 : rows + 8, at] = field[:, :, at] + UPDATE_RATE * (own[:, k, :rows] + top * landed[:, k, 8:])
        grid[:, rows + 8 :, at] = bottom * (edge[:, :, at] + UPDATE_RATE * (first[:, k] + own[:, k, rows:]))
    total = GRADIENT_SOFTEN
    pairs = []
    for part in (0, 1):
        u = grid[part]
        drow = pltpu.roll(u, u.shape[0] - 1, 0) - u
        dcol = pltpu.roll(u, u.shape[1] - 1, 1) - u
        total = total + drow * drow + dcol * dcol
        pairs.append((u, drow, dcol))
    inv = lax.rsqrt(total)
    for part, (u, drow, dcol) in enumerate(pairs):
        vrow, vcol = drow * inv, dcol * inv
        change = vrow - pltpu.roll(vrow, 1, 0) + vcol - pltpu.roll(vcol, 1, 1)
        out[part] = (u + SMOOTH_WEIGHT * change)[8 : rows + 8, :width]


def finish(spread, obj):
    rows, width = obj.shape[1:]
    tiles = width // LANES
    landed, before, first, beyond = exchange(spread, obj)
    hbm = pl.BlockSpec(memory_space=pl.ANY)
    return pl.pallas_call(
        smooth_kernel,
        out_shape=jax.ShapeDtypeStruct(obj.shape, F32),
        in_specs=[hbm] * 6,
        out_specs=pl.BlockSpec(memory_space=pltpu.VMEM),
        scratch_shapes=[
            pltpu.VMEM((2, rows + 16, width + LANES), F32),
            pltpu.VMEM((2, rows, width), F32),
            pltpu.VMEM((2, tiles, rows + 8, LANES), F32),
            pltpu.VMEM((2, 8, width), F32),
            pltpu.VMEM((2, tiles, rows + 8, LANES), F32),
            pltpu.VMEM((2, 8, width), F32),
            pltpu.VMEM((2, tiles, 8, LANES), F32),
            pltpu.SemaphoreType.DMA((6,)),
        ],
        compiler_params=pltpu.CompilerParams(vmem_limit_bytes=56 * 2**20),
    )(spread, obj, beyond, landed, before, first)


def per_device(object_field, probe, offsets, live, measured, gaps):
    spread = gradient(object_field, probe, offsets, live, measured, gaps)
    return finish(spread, object_field)


def solution(mesh):
    return jax.shard_map(
        per_device,
        mesh=mesh,
        in_specs=(
            P(None, "pos", None),
            P("mode", None, None, None),
            P("pos", None),
            P("pos"),
            P("pos", None, None),
            P(),
        ),
        out_specs=P(None, "pos", None),
        check_vma=False,
    )
```

time: 98.6 us -> 94.6 us (0.959)
  the two profiles are of different devices: /device:TPU:64 before, /device:TPU:32 now
where the time goes in v4:
time: 94.6 us; the launch traced here: 94.4 us
  Pallas kernels  94.4 us (100%)
    pallas_call x1, Pallas kernels, gradient(): pl.pallas_call(fused_kernel, out_shape=jax.ShapeDtypeStruct((2 * tiles, 2...  73.8 us
    pallas_call x1, Pallas kernels, exchange(): pl.pallas_call(tail_kernel, out_shape=(jax.ShapeDtypeStruct((2, tiles, ro...  17.3 us
    pallas_call x1, Pallas kernels, finish(): pl.pallas_call(smooth_kernel, out_shape=jax.ShapeDtypeStruct(obj.shape, F...  3.3 us

profile of v4, /device:TPU:32, one launch (start us, length us, event | category | flops | bytes accessed | tf_op | source)
XLA Modules:
  0.0 94.4 jit_solution(8566412257659074998)
XLA Ops:
  0.0 73.8 %shard_map.73 = f32[6,512,128]{2,1,0:T(8,128)} custom-call(s32[2,8]{1,0:T(2,128)} %bitcast.6, s32[8]{0:T(128)} %live.1, f32[2,256,384]{2,1,0:T(8,128)} %obj.5, f32[32,16,256]{2,1,0:T(8,128)} %bitcast.5, f32[8,256,256]{2,1,0:T(8,128)} %meas.1, s32[256,256]{1,0:T(8,128)} %gaps.1, bf16[9,256,256]{2,1,0:T(8,128)(2,1)} %constant.2.clone.tab), custom_call_target="tpu_custom_call" | custom-call | tf_op jit(solution)/shard_map/pallas_call | solution.py:306
  73.8 17.3 %shard_map.74 = (f32[2,3,264,128]{3,2,1,0:T(8,128)}, f32[2,8,384]{2,1,0:T(8,128)}, f32[2,3,8,128]{3,2,1,0:T(8,128)}, f32[2,8,384]{2,1,0:T(8,128)}) custom-call(f32[2,3,512,128]{3,2,1,0:T(8,128)} %bitcast.3, f32[2,256,384]{2,1,0:T(8,128)} %obj.5), custom_call_target="tpu_custom_call" | custom-call | tf_op jit(solution)/shard_map/pallas_call | solution.py:372
  91.1 3.3 %shard_map.75 = f32[2,256,384]{2,1,0:T(8,128)} custom-call(f32[2,3,512,128]{3,2,1,0:T(8,128)} %bitcast.4, f32[2,256,384]{2,1,0:T(8,128)} %obj.5, f32[2,8,384]{2,1,0:T(8,128)} %get-tuple-element.9.beyond, f32[2,3,264,128]{3,2,1,0:T(8,128)} %get-tuple-element.10.landed_, f32[2,8,384]{2,1,0:T(8,128)} %get-tuple-element.11.before_, ...), custom_call_target="tpu_custom_call" | custom-call | tf_op jit(solution)/shard_map/pallas_call | solution.py:427

commit v5 on v4

--- a/solution.py
+++ b/solution.py
@@ -98,8 +98,8 @@
 
 def fused_kernel(
     offsets, live, obj, probe, meas, gaps, tab,
-    out, acc, ext, probes, counts, holes, wave, patches, first, spec, ratio, mask, scr, wide,
-    sems, zs, zr, ps, pr, cs, cr, hs, hr,
+    base_out, landed, above, below, acc, ext, probes, counts, holes, wave, patches, first, spec, ratio, mask, scr, wide, base,
+    sems, zs, zr, ps, pr, cs, cr, hs, hr, ts, tr,
 ):
     slots, stripe = meas.shape[0], obj.shape[1]
     modes = probes.shape[0]
@@ -287,11 +287,20 @@
     forward(0)
     lax.fori_loop(0, slots - 1, visit, 0)
     inverse(slots - 1)
-    done = pltpu.make_async_copy(acc, out, sems.at[0])
+    tail = [send(acc.at[:, stripe:], landed, ts.at[0], tr.at[0], (after, mode))]
+    tail.append(send(acc.at[:, :8], below, ts.at[1], tr.at[1], (before, mode)))
+    for part in (0, 1):
+        for t in range(tiles):
+            at_ = part * tiles + t
+            base[at_] = ext[part, t, : stripe + 8] + UPDATE_RATE * acc[at_, : stripe + 8]
+    tail.append(send(base.at[:, stripe - 8 : stripe], above, ts.at[2], tr.at[2], (after, mode)))
+    done = pltpu.make_async_copy(base, base_out, sems.at[0])
     done.start()
     for copy in across + edge + spread + twin:
         copy.wait_send()
     done.wait()
+    for copy in tail:
+        copy.wait()
 
 
 def gradient(obj, probe, offsets, live, meas, gaps):
@@ -303,11 +312,12 @@
     pieces = probe.reshape(PLANE, -1, PATCH)
     smem, hbm = pl.BlockSpec(memory_space=pltpu.SMEM), pl.BlockSpec(memory_space=pl.ANY)
     vmem, dma = pltpu.VMEM, pltpu.SemaphoreType.DMA
-    spread = pl.pallas_call(
+    planes = lambda rows: jax.ShapeDtypeStruct((2 * tiles, rows, LANES), F32)
+    return pl.pallas_call(
         fused_kernel,
-        out_shape=jax.ShapeDtypeStruct((2 * tiles, 2 * stripe, LANES), F32),
+        out_shape=(planes(stripe + 8), planes(stripe), planes(8), planes(8)),
         in_specs=[smem] * 2 + [hbm] * 5,
-        out_specs=hbm,
+        out_specs=[hbm] * 4,
         scratch_shapes=[
             vmem((2 * tiles, 2 * stripe, LANES), F32),
             vmem((2, tiles, 2 * stripe, LANES), F32),
@@ -322,6 +332,7 @@
             vmem((PATCH, PATCH), F32),
             vmem((2, PATCH, HALF), F32),
             vmem((2, tiles, 3 * stripe, LANES), F32),
+            vmem((2 * tiles, stripe + 8, LANES), F32),
             dma((4 + tiles,)),
             dma((modes - 1,)),
             dma((modes - 1,)),
@@ -331,79 +342,34 @@
             dma((CHIPS,)),
             dma((tiles,)),
             dma((tiles,)),
+            dma((3,)),
+            dma((3,)),
         ],
         compiler_params=pltpu.CompilerParams(
             collective_id=0, has_side_effects=True, vmem_limit_bytes=60 * 2**20
         ),
     )(offsets.T, live, obj, pieces, meas, gaps, tab)
-    return spread.reshape(2, tiles, 2 * stripe, LANES)
-
-
-def tail_kernel(spread, obj, landed, before, first, beyond, ss, rs):
-    me, mode = lax.axis_index("pos"), lax.axis_index("mode")
-    size, rows = lax.axis_size("pos"), obj.shape[1]
-    previous, following = (me + size - 1) % size, (me + 1) % size
-    barrier = pltpu.get_barrier_semaphore()
-    for q in (previous, following):
-        pl.semaphore_signal(barrier, inc=1, device_id=(q, mode), device_id_type=MESH)
-    pl.semaphore_wait(barrier, 2)
-    far = [
-        (spread.at[:, :, rows - 8 :], landed, following),
-        (obj.at[:, rows - 8 :], before, following),
-        (spread.at[:, :, :8], first, previous),
-        (obj.at[:, :8], beyond, previous),
-    ]
-    far = [
-        pltpu.make_async_remote_copy(
-            src_ref=src, dst_ref=dst, send_sem=ss.at[k], recv_sem=rs.at[k], device_id=(q, mode), device_id_type=MESH
-        )
-        for k, (src, dst, q) in enumerate(far)
-    ]
-    for copy in far:
-        copy.start()
-    for copy in far:
-        copy.wait()
-
-
-def exchange(spread, obj):
-    rows, width = obj.shape[1:]
+
+
+def smooth_kernel(base_, landed_, above_, below_, out, grid, base, landed, above, below, sems):
+    rows, width = out.shape[1:]
     tiles = width // LANES
-    hbm, dma = pl.BlockSpec(memory_space=pl.ANY), pltpu.SemaphoreType.DMA
-    return pl.pallas_call(
-        tail_kernel,
-        out_shape=(
-            jax.ShapeDtypeStruct((2, tiles, rows + 8, LANES), F32),
-            jax.ShapeDtypeStruct((2, 8, width), F32),
-            jax.ShapeDtypeStruct((2, tiles, 8, LANES), F32),
-            jax.ShapeDtypeStruct((2, 8, width), F32),
-        ),
-        in_specs=[hbm] * 2,
-        out_specs=[hbm] * 4,
-        scratch_shapes=[dma((4,)), dma((4,))],
-        compiler_params=pltpu.CompilerParams(collective_id=1, has_side_effects=True),
-    )(spread, obj)
-
-
-def smooth_kernel(spread, obj, beyond, landed_, before_, first_, out, grid, field, own, edge, landed, before, first, sems):
-    rows, width = obj.shape[1:]
     me, size = lax.axis_index("pos"), lax.axis_size("pos")
-    near = [
-        (landed_, landed), (spread.at[:, :, : rows + 8], own), (obj, field),
-        (beyond, edge), (before_, before), (first_, first),
-    ]
+    near = [(base_, base), (landed_, landed), (above_, above), (below_, below)]
     near = [pltpu.make_async_copy(src, dst, sems.at[k]) for k, (src, dst) in enumerate(near)]
     for copy in near:
         copy.start()
-    grid[...] = jnp.zeros_like(grid)
+    grid[:, :, width:] = jnp.zeros((2, rows + 16, LANES), F32)
     for copy in near:
         copy.wait()
     top = jnp.where(me > 0, 1.0, 0.0)
     bottom = jnp.where(me < size - 1, 1.0, 0.0)
-    for k in range(width // LANES):
-        at = slice(LANES * k, LANES * (k + 1))
-        grid[:, 0:8, at] = top * (before[:, :, at] + UPDATE_RATE * landed[:, k, :8])
-        grid[:, 8 : rows + 8, at] = field[:, :, at] + UPDATE_RATE * (own[:, k, :rows] + top * landed[:, k, 8:])
-        grid[:, rows + 8 :, at] = bottom * (edge[:, :, at] + UPDATE_RATE * (first[:, k] + own[:, k, rows:]))
+    for part in (0, 1):
+        for t in range(tiles):
+            at, k = slice(LANES * t, LANES * (t + 1)), part * tiles + t
+            grid[part, 0:8, at] = top * above[k]
+            grid[part, 8 : rows + 8, at] = base[k, :rows] + (UPDATE_RATE * top) * landed[k]
+            grid[part, rows + 8 :, at] = bottom * (base[k, rows:] + UPDATE_RATE * below[k])
     total = GRADIENT_SOFTEN
     pairs = []
     for part in (0, 1):
@@ -419,33 +385,23 @@
         out[part] = (u + SMOOTH_WEIGHT * change)[8 : rows + 8, :width]
 
 
-def finish(spread, obj):
-    rows, width = obj.shape[1:]
-    tiles = width // LANES
-    landed, before, first, beyond = exchange(spread, obj)
+def finish(shape, parts):
+    rows, width = shape[1:]
     hbm = pl.BlockSpec(memory_space=pl.ANY)
     return pl.pallas_call(
         smooth_kernel,
-        out_shape=jax.ShapeDtypeStruct(obj.shape, F32),
-        in_specs=[hbm] * 6,
+        out_shape=jax.ShapeDtypeStruct(shape, F32),
+        in_specs=[hbm] * 4,
         out_specs=pl.BlockSpec(memory_space=pltpu.VMEM),
-        scratch_shapes=[
-            pltpu.VMEM((2, rows + 16, width + LANES), F32),
-            pltpu.VMEM((2, rows, width), F32),
-            pltpu.VMEM((2, tiles, rows + 8, LANES), F32),
-            pltpu.VMEM((2, 8, width), F32),
-            pltpu.VMEM((2, tiles, rows + 8, LANES), F32),
-            pltpu.VMEM((2, 8, width), F32),
-            pltpu.VMEM((2, tiles, 8, LANES), F32),
-            pltpu.SemaphoreType.DMA((6,)),
-        ],
+        scratch_shapes=[pltpu.VMEM((2, rows + 16, width + LANES), F32)]
+        + [pltpu.VMEM(x.shape, F32) for x in parts]
+        + [pltpu.SemaphoreType.DMA((4,))],
         compiler_params=pltpu.CompilerParams(vmem_limit_bytes=56 * 2**20),
-    )(spread, obj, beyond, landed, before, first)
+    )(*parts)
 
 
 def per_device(object_field, probe, offsets, live, measured, gaps):
-    spread = gradient(object_field, probe, offsets, live, measured, gaps)
-    return finish(spread, object_field)
+    return finish(object_field.shape, gradient(object_field, probe, offsets, live, measured, gaps))
 
 
 def solution(mesh):

time: 94.6 us -> 89 us (0.941)
  Pallas kernels: 94.4 us -> 88.8 us
    pallas_call x3 -> x2, Pallas kernels: 94.4 us -> 88.8 us  [the longest x1 85.8 us: gradient(): pl.pallas_call(fused_kernel, out_shape=(planes(stripe + 8), planes(stripe...]
where the time goes in v5:
time: 89 us; the launch traced here: 88.8 us
  Pallas kernels  88.8 us (100%)
    pallas_call x1, Pallas kernels, gradient(): pl.pallas_call(fused_kernel, out_shape=(planes(stripe + 8), planes(stripe...  85.8 us
    pallas_call x1, Pallas kernels, finish(): pl.pallas_call(smooth_kernel, out_shape=jax.ShapeDtypeStruct(shape, F32),...  3.01 us

profile of v5, /device:TPU:32, one launch (start us, length us, event | category | flops | bytes accessed | tf_op | source)
XLA Modules:
  0.0 88.8 jit_solution(16000781143413318348)
XLA Ops:
  0.0 85.8 %shard_map.73 = (f32[6,264,128]{2,1,0:T(8,128)}, f32[6,256,128]{2,1,0:T(8,128)}, f32[6,8,128]{2,1,0:T(8,128)}, f32[6,8,128]{2,1,0:T(8,128)}) custom-call(s32[2,8]{1,0:T(2,128)} %bitcast.3, s32[8]{0:T(128)} %live.1, f32[2,256,384]{2,1,0:T(8,128)} %obj.1, f32[32,16,256]{2,1,0:T(8,128)} %bitcast.2, f32[8,256,256]{2,1,0:T(8,128)} %meas.1, s32[256,256]{1,0:T(8,128)} %gaps.1, ...), custom_call_target="tpu_custom_call" | custom-call | tf_op jit(solution)/shard_map/pallas_call | solution.py:316
  85.8 3.0 %shard_map.74 = f32[2,256,384]{2,1,0:T(8,128)} custom-call(f32[6,264,128]{2,1,0:T(8,128)} %get-tuple-element.9.base_, f32[6,256,128]{2,1,0:T(8,128)} %get-tuple-element.10.landed_, f32[6,8,128]{2,1,0:T(8,128)} %get-tuple-element.11.above_, f32[6,8,128]{2,1,0:T(8,128)} %get-tuple-element.12.below_), custom_call_target="tpu_custom_call" | custom-call | tf_op jit(solution)/shard_map/pallas_call | solution.py:391

commit v6 on v5

--- a/solution.py
+++ b/solution.py
@@ -125,8 +125,9 @@
         return ((chip + k) % CHIPS) * 2 + core
 
     barrier = pltpu.get_barrier_semaphore()
-    peers = [(me, (mode + d) % modes) for d in range(1, modes)]
-    peers += [(plane + at(k), mode) for k in range(1, CHIPS)]
+    mirror = size - PLANE - plane + lane_of
+    partners = [(me, (mode + 1) % modes), (me, (mode + 3) % modes), (mirror, (mode + 2) % modes)]
+    peers = partners + [(plane + at(k), mode) for k in range(1, CHIPS)]
     peers += [(q, mode) for q in (sibling, before, after)]
     for peer in peers:
         pl.semaphore_signal(barrier, inc=1, device_id=peer, device_id_type=MESH)
@@ -140,8 +141,8 @@
         return copy
 
     across = [
-        send(probe.at[lane_of], probes.at[modes - d, lane_of], zs.at[d - 1], zr.at[d - 1], (me, (mode + d) % modes))
-        for d in range(1, modes)
+        send(probe.at[lane_of], probes.at[k + 1, lane_of], zs.at[k], zr.at[k], peer)
+        for k, peer in enumerate(partners)
     ]
     edge = [
         send(obj.at[:, :, cols(t)], ext.at[:, t, stripe:], hs.at[t], hr.at[t], (before, mode)) for t in range(tiles)
@@ -237,11 +238,13 @@
             first[g * BATCH + k, 1] = o
         return carry
 
-    lax.fori_loop(0, slots // BATCH, own, 0)
+    own(0, 0)
 
     for k in range(1, CHIPS):
         spread[CHIPS - k - 1].wait_recv()
         twin.append(send(block(k), block(k), cs.at[k], cr.at[k], (sibling, mode)))
+    for g in range(1, slots // BATCH):
+        own(g, 0)
     for copy in twin:
         copy.wait_recv()
 
@@ -351,7 +354,7 @@
     )(offsets.T, live, obj, pieces, meas, gaps, tab)
 
 
-def smooth_kernel(base_, landed_, above_, below_, out, grid, base, landed, above, below, sems):
+def smooth_kernel(base_, landed_, above_, below_, result, out, grid, base, landed, above, below, sems):
     rows, width = out.shape[1:]
     tiles = width // LANES
     me, size = lax.axis_index("pos"), lax.axis_size("pos")
@@ -379,10 +382,15 @@
         total = total + drow * drow + dcol * dcol
         pairs.append((u, drow, dcol))
     inv = lax.rsqrt(total)
+    leaving = []
     for part, (u, drow, dcol) in enumerate(pairs):
         vrow, vcol = drow * inv, dcol * inv
         change = vrow - pltpu.roll(vrow, 1, 0) + vcol - pltpu.roll(vcol, 1, 1)
         out[part] = (u + SMOOTH_WEIGHT * change)[8 : rows + 8, :width]
+        leaving.append(pltpu.make_async_copy(out.at[part], result.at[part], sems.at[part]))
+        leaving[part].start()
+    for copy in leaving:
+        copy.wait()
 
 
 def finish(shape, parts):
@@ -392,8 +400,8 @@
         smooth_kernel,
         out_shape=jax.ShapeDtypeStruct(shape, F32),
         in_specs=[hbm] * 4,
-        out_specs=pl.BlockSpec(memory_space=pltpu.VMEM),
-        scratch_shapes=[pltpu.VMEM((2, rows + 16, width + LANES), F32)]
+        out_specs=hbm,
+        scratch_shapes=[pltpu.VMEM(shape, F32), pltpu.VMEM((2, rows + 16, width + LANES), F32)]
         + [pltpu.VMEM(x.shape, F32) for x in parts]
         + [pltpu.SemaphoreType.DMA((4,))],
         compiler_params=pltpu.CompilerParams(vmem_limit_bytes=56 * 2**20),

time: 89 us -> 88.4 us (level)
  no operation moved by 1% of the time
where the time goes in v6:
time: 88.4 us; the launch traced here: 88.3 us
  Pallas kernels  88.2 us (100%)
    pallas_call x1, Pallas kernels, gradient(): pl.pallas_call(fused_kernel, out_shape=(planes(stripe + 8), planes(stripe...  85.3 us
    pallas_call x1, Pallas kernels, finish(): pl.pallas_call(smooth_kernel, out_shape=jax.ShapeDtypeStruct(shape, F32),...  2.87 us

profile of v6, /device:TPU:32, one launch (start us, length us, event | category | flops | bytes accessed | tf_op | source)
XLA Modules:
  0.0 88.3 jit_solution(3830110008691177867)
XLA Ops:
  0.0 85.3 %shard_map.73 = (f32[6,264,128]{2,1,0:T(8,128)}, f32[6,256,128]{2,1,0:T(8,128)}, f32[6,8,128]{2,1,0:T(8,128)}, f32[6,8,128]{2,1,0:T(8,128)}) custom-call(s32[2,8]{1,0:T(2,128)} %bitcast.3, s32[8]{0:T(128)} %live.1, f32[2,256,384]{2,1,0:T(8,128)} %obj.1, f32[32,16,256]{2,1,0:T(8,128)} %bitcast.2, f32[8,256,256]{2,1,0:T(8,128)} %meas.1, s32[256,256]{1,0:T(8,128)} %gaps.1, ...), custom_call_target="tpu_custom_call" | custom-call | tf_op jit(solution)/shard_map/pallas_call | solution.py:319
  85.3 2.9 %shard_map.74 = f32[2,256,384]{2,1,0:T(8,128)} custom-call(f32[6,264,128]{2,1,0:T(8,128)} %get-tuple-element.9.base_, f32[6,256,128]{2,1,0:T(8,128)} %get-tuple-element.10.landed_, f32[6,8,128]{2,1,0:T(8,128)} %get-tuple-element.11.above_, f32[6,8,128]{2,1,0:T(8,128)} %get-tuple-element.12.below_), custom_call_target="tpu_custom_call" | custom-call | tf_op jit(solution)/shard_map/pallas_call | solution.py:399
